TPU v7x, 128 devices: a whole 4x4x4 slice. The times are simulated.
128 devices in a mesh: tm: 8 (over z, core), tile: 16 (over x, y).
Axes of the slice: x: 4, y: 4, z: 4, core: 2. Of those that a mesh axis runs over, the one named last changes fastest.
Arguments:
- pix_grad: bfloat16 [128, 3, 256, 320], P(('tm', 'tile')), may hold values from -6 to 6
- frame_ids: int32 [128], P(('tm', 'tile')), may hold values from 0 to 15
- pre_norm: bfloat16 [16, 256, 30720], P('tm', None, 'tile'), may hold values from -6 to 6
- group_norm_gain: float32 [96], replicated, may hold values from 0.1 to 1.9
- group_norm_bias: float32 [96], replicated, may hold values from -3 to 3
- out_weight: bfloat16 [96, 3], replicated, may hold values from -0.625 to 0.625
- conv_weight: bfloat16 [27, 96, 384], replicated, may hold values from -0.0625 to 0.0625
- in_weight: bfloat16 [16, 384], replicated, may hold values from -1.5 to 1.5
Outputs:
- latent_grad: float32 [1024, 5120], P(('tm', 'tile'))
All inputs are finite; a program needn't handle non-finite values.
Results may differ from a plain program's by a relative error of at most 0.0029.
Values may be sent and summed in bfloat16 or wider, within the bound.
A program may use at most 320 MiB of HBM per device.

v0:
```python
import jax
import jax.numpy as jnp
from jax import lax
from jax.sharding import PartitionSpec as P

NORM_GROUPS = 32


def extended(shard, sides, width):
    for axis, dim in sides:
        size, length = (lax.axis_size(axis), shard.shape[dim])
        up = [(i, (i + 1) % size) for i in range(size - 1)]
        down = [(j, i) for i, j in up]
        last = lax.slice_in_dim(shard, length - width, length, axis=dim)
        initial = lax.slice_in_dim(shard, 0, width, axis=dim)
        before = lax.ppermute(last, axis, up)
        after = lax.ppermute(initial, axis, down)
        shard = jnp.concatenate([before, shard, after], axis=dim)
    return shard


def passed_along(shard, axis, by):
    size = lax.axis_size(axis)
    pairs = [(i, i + by) for i in range(size) if 0 <= i + by < size]
    return lax.ppermute(shard, axis, pairs)


def pool_project(dup, in_weight):
    frames_here, output_rows, strip_columns, in_chans = dup.shape
    dfeat = dup.reshape(frames_here, output_rows // 2, 2, strip_columns // 2, 2, in_chans).sum(
        axis=(2, 4)
    )
    return jnp.einsum(
        "fijc,lc->fijl", dfeat, in_weight.astype(jnp.float32), precision=lax.Precision.HIGHEST
    )


def body(
    pix_grad,
    frame_ids,
    pre_norm,
    group_norm_gain,
    group_norm_bias,
    out_weight,
    conv_weight,
    in_weight,
):
    highest = lax.Precision.HIGHEST
    n_time = lax.axis_size("tm")
    n_strip = lax.axis_size("tile")
    frame_extent, output_rows, merged = pre_norm.shape
    channel_count = group_norm_gain.shape[0]
    strip_columns = merged // channel_count
    frames = frame_extent * n_time
    held = pix_grad.shape[0]
    onehot = (frame_ids[None, :] == jnp.arange(frames, dtype=jnp.int32)[:, None]).astype(
        jnp.bfloat16
    )
    spread = jnp.dot(onehot, pix_grad.reshape(held, -1), preferred_element_type=jnp.float32)
    spread = spread.reshape(n_time, frame_extent, 3, output_rows, n_strip, strip_columns).transpose(
        0, 4, 1, 2, 3, 5
    )
    spread = spread.reshape(n_time * n_strip * frame_extent, 3, output_rows, strip_columns)
    dpix = lax.psum_scatter(spread, ("tm", "tile"), scatter_dimension=0, tiled=True)
    x = pre_norm.astype(jnp.float32).reshape(
        frame_extent, output_rows, strip_columns, channel_count
    )
    da = jnp.einsum("fkhw,mk->fhwm", dpix, out_weight.astype(jnp.float32), precision=highest)
    grouped_input = x.reshape(
        frame_extent, output_rows, strip_columns, NORM_GROUPS, channel_count // NORM_GROUPS
    )
    count = output_rows * strip_columns * n_strip * (channel_count // NORM_GROUPS)
    totals, squares = lax.psum(
        (
            jnp.sum(grouped_input, axis=(1, 2, 4)),
            jnp.sum(grouped_input * grouped_input, axis=(1, 2, 4)),
        ),
        "tile",
    )
    group_mean = (totals / count)[:, None, None, :, None]
    meansq = (squares / count)[:, None, None, :, None]
    inverse_deviation = lax.rsqrt(meansq - group_mean * group_mean + 1e-05)
    normalized_input = ((grouped_input - group_mean) * inverse_deviation).reshape(
        frame_extent, output_rows, strip_columns, channel_count
    )
    norm_output = normalized_input * group_norm_gain + group_norm_bias
    sig = jax.nn.sigmoid(norm_output)
    dxh = (da * sig * (1.0 + norm_output * (1.0 - sig)) * group_norm_gain).reshape(
        frame_extent, output_rows, strip_columns, NORM_GROUPS, channel_count // NORM_GROUPS
    )
    grouped_normalized = normalized_input.reshape(
        frame_extent, output_rows, strip_columns, NORM_GROUPS, channel_count // NORM_GROUPS
    )
    first, second = lax.psum(
        (jnp.sum(dxh, axis=(1, 2, 4)), jnp.sum(dxh * grouped_normalized, axis=(1, 2, 4))), "tile"
    )
    first = (first / count)[:, None, None, :, None]
    second = (second / count)[:, None, None, :, None]
    dconv = (
        (inverse_deviation * (dxh - first - grouped_normalized * second))
        .reshape(frame_extent, output_rows, strip_columns, channel_count)
        .astype(jnp.bfloat16)
    )
    widened = extended(dconv, (("tile", 2),), 1)
    in_chans = conv_weight.shape[2]
    weights = conv_weight.reshape(27 * channel_count, in_chans)
    following = passed_along(widened, "tm", -1)
    stacked = jnp.concatenate([widened, following], axis=0)
    stacked = jnp.pad(stacked, ((0, 0), (1, 1), (0, 0), (0, 0)))
    pieces = []
    for tdel in range(3):
        for hdel in range(3):
            for wdel in range(3):
                pieces.append(
                    stacked[
                        2 - tdel : 2 - tdel + frame_extent,
                        2 - hdel : 2 - hdel + output_rows,
                        2 - wdel : 2 - wdel + strip_columns,
                    ]
                )
    cols = jnp.concatenate(pieces, axis=-1).reshape(
        frame_extent * output_rows * strip_columns, 27 * channel_count
    )
    dup = jnp.dot(cols, weights, preferred_element_type=jnp.float32).reshape(
        frame_extent, output_rows, strip_columns, in_chans
    )
    dlat = pool_project(dup, in_weight)
    latent = in_weight.shape[0]
    half_rows = output_rows // 4
    half_cols = strip_columns // 4
    tokens = dlat.reshape(frame_extent, half_rows, 2, half_cols, 2, latent).transpose(
        0, 1, 3, 5, 2, 4
    )
    tokens = tokens.reshape(frame_extent * half_rows, half_cols, latent * 4)
    placed = lax.all_to_all(tokens, "tile", split_axis=0, concat_axis=1, tiled=True)
    return placed.reshape(placed.shape[0], -1)


def solution(mesh):
    return jax.shard_map(
        body,
        mesh=mesh,
        in_specs=(
            P(("tm", "tile"), None, None, None),
            P(("tm", "tile")),
            P("tm", None, "tile"),
            P(),
            P(),
            P(),
            P(),
            P(),
        ),
        out_specs=P(("tm", "tile"), None),
        check_vma=False,
    )
```

profile of v0, /device:TPU:1, one launch (start us, length us, event | category | flops | bytes accessed | tf_op | source)
XLA Modules:
  0.0 603.2 jit_solution(12950291553064236827)
XLA Ops:
  6.5 1.3 reshape.86
  8.5 9.0 %broadcast_multiply_fusion = f32[8,2,3,256,16,20]{3,5,2,1,4,0:T(8,128)} fusion(f32[8,2]{1,0:T(8,128)S(1)} %reshape.85, f32[3,256,16,20]{1,3,2,0:T(8,128)S(1)} %reshape.86), kind=kLoop, calls=%fused_computation.20 | loop fusion | flops 3932160 | bytes 16711744 | tf_op jit(solution)/shard_map/dot_general | solution.py:59
  17.6 4.2 copy.22
  21.8 2.1 multiply_reduce_fusion.1
  25.2 34.2 %all-reduce.2 = (f32[2,32]{1,0:T(2,128)S(1)}, f32[2,32]{1,0:T(2,128)S(1)}) all-reduce(f32[2,32]{1,0:T(2,128)S(1)} %reduce_sum.62, f32[2,32]{1,0:T(2,128)S(1)} %reduce_sum.59), channel_id=1, replica_groups=mesh['tm'=8,'tile'=16] {'tile'}, use_global_device_ids=true, to_apply=%region_5.0 | all-reduce | flops 128 | bytes 1024 | tf_op jit(solution)/shard_map/psum | solution.py:73
  59.8 196.0 %reduce-scatter.2.cloned.1.call-done = f32[2,3,256,20]{2,3,1,0:T(8,128)} async-done(((f32[256,3,256,20]{2,3,1,0:T(8,128)}), f32[2,3,256,20]{2,3,1,0:T(8,128)}) %reduce-scatter.2.cloned.1.call-update) | async-done | bytes 122896 | tf_op jit(solution)/shard_map/reduce_scatter | solution.py:64
  255.8 7.8 %fusion.33 = (f32[2,96]{1,0:T(2,128)S(1)}, f32[2,96]{1,0:T(2,128)S(1)}, f32[2,256,20,96]{1,3,2,0:T(8,128)}) fusion(f32[2,96]{1,0:T(2,128)S(1)} %mul.73, f32[2,256,20,96]{1,3,2,0:T(8,128)} %bitcast.40, f32[2,96]{1,0:T(2,128)S(1)} %sub.41, f32[96]{0:T(128)S(1)} %copy-done.3, f32[96]{0:T(128)S(1)} %copy-done.4, bf16[96,3]{0,1:T(4,128)(2,1)S(1)} %copy-done.2, ...), kind=kOutput, calls=%fused_computation.70 | convolution fusion | flops 51117696 | bytes 7991616 | tf_op jit(solution)/shard_map/fkhw,mk->fhwm/dot_general | solution.py:68
  264.0 30.9 %all-reduce.1 = (f32[2,32]{1,0:T(2,128)S(1)}, f32[2,32]{1,0:T(2,128)S(1)}) all-reduce(f32[2,32]{1,0:T(2,128)S(1)} %reduce_sum.84, f32[2,32]{1,0:T(2,128)S(1)} %reduce_sum.81), channel_id=1, replica_groups=mesh['tm'=8,'tile'=16] {'tile'}, use_global_device_ids=true, to_apply=%region_12.13 | all-reduce | flops 128 | bytes 1024 | tf_op jit(solution)/shard_map/psum | solution.py:94
  295.3 4.4 multiply_convert_fusion
  299.8 1.3 collective-permute-start
  301.1 1.3 collective-permute-start.1
  302.7 3.7 collective-permute-done.1
  306.7 12.8 %collective-permute-start.2 = (bf16[2,256,22,96]{1,3,2,0:T(8,128)(2,1)S(1)}, bf16[2,256,22,96]{1,3,2,0:T(8,128)(2,1)S(1)}, u32[]{:S(2)}, u32[]{:S(2)}) collective-permute-start(bf16[2,256,22,96]{1,3,2,0:T(8,128)(2,1)S(1)} %pad_maximum_fusion.1), channel_id=1, source_target_pairs={{16,0},{32,16},{48,32},{64,48},{80,64},{96,80},{112,96},{17,1},{33... | collective-permute-start | bytes 6488072 | tf_op jit(solution)/shard_map/ppermute | solution.py:25
  319.6 24.2 %collective-permute-done.2 = bf16[2,256,22,96]{1,3,2,0:T(8,128)(2,1)S(1)} collective-permute-done((bf16[2,256,22,96]{1,3,2,0:T(8,128)(2,1)S(1)}, bf16[2,256,22,96]{1,3,2,0:T(8,128)(2,1)S(1)}, u32[]{:S(2)}, u32[]{:S(2)}) %collective-permute-start.2) | collective-permute-done | bytes 2162720 | tf_op jit(solution)/shard_map/ppermute | solution.py:25
  344.5 2.0 fusion.7
  346.5 2.3 fusion.8
  348.8 2.2 fusion.9
  351.0 1.5 slice_dynamic-update-slice_fusion.5
  352.5 1.4 slice_dynamic-update-slice_fusion.4
  353.9 1.4 slice_dynamic-update-slice_fusion.3
  355.3 2.3 fusion.10
  357.6 2.2 fusion.11
  359.8 2.3 fusion.12
  362.1 2.3 fusion.13
  364.3 2.3 fusion.14
  366.7 2.3 fusion.15
  369.0 1.4 slice_dynamic-update-slice_fusion.2
  370.4 1.4 slice_dynamic-update-slice_fusion.1
  371.8 1.4 slice_dynamic-update-slice_fusion
  373.2 2.2 fusion.16
  375.5 2.3 fusion.17
  377.8 2.3 fusion.18
  380.1 2.4 fusion.19
  382.5 2.3 fusion.20
  384.8 2.2 fusion.21
  387.0 1.4 fusion.26
  388.5 1.4 constant_dynamic-update-slice_fusion
  389.9 1.4 fusion.25
  391.3 2.3 fusion.22
  393.6 2.3 fusion.23
  395.9 2.3 fusion.24
  398.2 133.3 %copy.23 = bf16[2,256,20,2592]{3,0,2,1:T(2,128)(2,1)} copy(bf16[2,256,20,2592]{1,3,2,0:T(8,128)(2,1)} %fusion.24) | data formatting | bytes 106168320 | tf_op jit(solution)/shard_map/concatenate | solution.py:121
  531.5 44.5 %fusion.4 = f32[2,128,10,384]{3,1,2,0:T(8,128)S(1)} fusion(bf16[2592,384,1,1,1,1]{1,0,5,4,3,2:T(8,128)(2,1)S(1)} %bitcast.37, bf16[2,128,2,10,2,2592]{5,0,4,3,2,1:T(2,128)(2,1)} %bitcast.39), kind=kOutput, calls=%fused_computation.29 | convolution fusion | flops 20387266560 | bytes 59006976 | tf_op jit(solution)/shard_map/dot_general | solution.py:124
  576.0 3.0 copy.25
  579.1 3.2 fusion.27
  583.3 10.0 %all_to_all.15 = f32[16,1,2560]{2,1,0:T(1,128)S(1)} all-to-all(f32[16,1,2560]{2,1,0:T(1,128)S(1)} %reshape.90), channel_id=1, replica_groups=mesh['tm'=8,'tile'=16] {'tile'}, dimensions={0} | all-to-all | bytes 327680 | tf_op jit(solution)/shard_map/all_to_all | solution.py:135
  593.8 1.0 reduce.8
  595.0 0.8 reshape.84
  (43 shorter events, 5.5 us)
Async XLA Ops:
  6.5 525.0 %copy-start = (bf16[27,96,384]{2,1,0:T(8,128)(2,1)S(1)}, bf16[27,96,384]{2,1,0:T(8,128)(2,1)}, u32[]{:S(2)}) copy-start(bf16[27,96,384]{2,1,0:T(8,128)(2,1)} %param.14) | copy-start | bytes 5971972
  6.5 249.3 %reduce-scatter.2.cloned.1.call-start = ((), (), s32[]{:S(2)}) async-start(), calls=%async_computation.2 | async-start | bytes 19021824 | tf_op jit(solution)/shard_map/reduce_scatter | solution.py:64
  17.5 238.3 %copy-start.2 = (bf16[96,3]{0,1:T(4,128)(2,1)S(1)}, bf16[96,3]{0,1:T(4,128)(2,1)}, u32[]{:S(2)}) copy-start(bf16[96,3]{0,1:T(4,128)(2,1)} %param.13) | copy-start | bytes 1732
  17.5 238.3 %copy-start.3 = (f32[96]{0:T(128)S(1)}, f32[96]{0:T(128)}, u32[]{:S(2)}) copy-start(f32[96]{0:T(128)} %param.12) | copy-start | bytes 1156
  17.6 238.2 %copy-start.4 = (f32[96]{0:T(128)S(1)}, f32[96]{0:T(128)}, u32[]{:S(2)}) copy-start(f32[96]{0:T(128)} %param.11) | copy-start | bytes 1156
  299.8 2.9 collective-permute-start
  301.1 5.4 collective-permute-start.1
  306.7 37.0 %collective-permute-start.2 = (bf16[2,256,22,96]{1,3,2,0:T(8,128)(2,1)S(1)}, bf16[2,256,22,96]{1,3,2,0:T(8,128)(2,1)S(1)}, u32[]{:S(2)}, u32[]{:S(2)}) collective-permute-start(bf16[2,256,22,96]{1,3,2,0:T(8,128)(2,1)S(1)} %pad_maximum_fusion.1), channel_id=1, source_target_pairs={{16,0},{32,16},{48,32},{64,48},{80,64},{96,80},{112,96},{17,1},{33... | collective-permute-start | bytes 6488072 | tf_op jit(solution)/shard_map/ppermute | solution.py:25
  576.0 3.1 copy-start.1
Sparse Core Ops, SparseCore 0:
  17.7 238.0 reduce-scatter.1
where the time goes:
time: 614 us; the launch traced here: 603 us
  waiting for transfers between devices  224 us (36%)
  local copies, waits for them, and re-layouts  197 us (32%)
  blocking collectives  75.2 us (12%)
  matrix products  55.5 us (9%)
  other arithmetic  20.8 us (3%)
  starting transfers between devices  15.4 us (3%)
  between operations  14.8 us (2%)
    reduce_scatter x1, waiting for transfers between devices, body(): lax.psum_scatter(spread, ('tm', 'tile'), scatter_dimension=0, tiled=True)  196 us
    concatenate x2, local copies, waits for them, and re-layouts, body(): jnp.concatenate(pieces, axis=-1)  136 us
    unnamed x36, local copies, waits for them, and re-layouts  49 us
    dot_general x1, matrix products, body(): jnp.dot(cols, weights, preferred_element_type=jnp.float32)  44.5 us
    psum x1, blocking collectives, body(): lax.psum((jnp.sum(grouped_input, axis=(1, 2, 4)), jnp.sum(grouped_input *...  34.2 us
    psum x1, blocking collectives, body(): lax.psum((jnp.sum(dxh, axis=(1, 2, 4)), jnp.sum(dxh * grouped_normalized,...  30.9 us
    ppermute x1, waiting for transfers between devices, passed_along(): return lax.ppermute(shard, axis, pairs)  24.2 us
    ppermute x1, starting transfers between devices, passed_along(): return lax.ppermute(shard, axis, pairs)  12.8 us
  transfers between devices with their start and end apart: 4, of which 4 were waited for; matrix products, arithmetic and copies ran while one was open for 1% of the time, Pallas kernels for 0%

commit v1 on v0

v1 whole, which is shorter than its diff:
```python
import functools

import jax
import jax.numpy as jnp
from jax import lax
from jax.experimental import pallas as pl
from jax.experimental.pallas import tpu as pltpu
from jax.sharding import PartitionSpec as P

MESH = pl.DeviceIdType.MESH
F32 = jnp.float32
BF16 = jnp.bfloat16
HIGHEST = lax.Precision.HIGHEST
COUNT = 256.0 * 320.0 * 3.0
EPS = 1e-05
BLK = 384
PIECES = 10


def iota(shape, dim):
    return lax.broadcasted_iota(jnp.int32, shape, dim)


def remote(src, dst, send_sem, recv_sem, device):
    return pltpu.make_async_remote_copy(
        src_ref=src,
        dst_ref=dst,
        send_sem=send_sem,
        recv_sem=recv_sem,
        device_id=device,
        device_id_type=MESH,
    )


def kernel(
    pix_hbm,
    fid,
    x_hbm,
    gain,
    bias,
    ow,
    cw_hbm,
    iw,
    out,
    pixv,
    xb,
    cwv,
    sbuf,
    rbuf,
    sums,
    cbuf,
    part,
    zbuf,
    dpx,
    rmat,
    xs,
    fs,
    gmat,
    emat,
    stin,
    stsend,
    strecv,
    cst,
    gred,
    bmat,
    lhs,
    ys,
    tok,
    trecv,
    pix_sem,
    x_sem,
    cw_sem,
    s1s,
    s1r,
    cs,
    cr,
    zs,
    zr,
    sts,
    strs,
    tks,
    tkr,
):
    tm = lax.axis_index("tm")
    tl = lax.axis_index("tile")
    z = lax.div(tm, 2)
    c = lax.rem(tm, 2)
    below = lax.rem(tm + 7, 8)
    above = lax.rem(tm + 1, 8)

    pix_cp = pltpu.make_async_copy(pix_hbm.at[0], pixv, pix_sem)
    pix_cp.start()
    x_cps = []
    for f in range(2):
        for b in range(5):
            cp = pltpu.make_async_copy(
                x_hbm.at[f, :, pl.ds(BLK * b, BLK)], xb.at[f * 5 + b], x_sem.at[f * 5 + b]
            )
            cp.start()
            x_cps.append(cp)
    cw_cp = pltpu.make_async_copy(cw_hbm, cwv, cw_sem)
    cw_cp.start()

    barrier = pltpu.get_barrier_semaphore()

    def greet(device):
        pl.semaphore_signal(barrier, inc=1, device_id=device, device_id_type=MESH)

    def greet_tile(d, _):
        j = lax.rem(tl + d, 16)
        greet((tm, j))
        return 0

    lax.fori_loop(1, 16, greet_tile, 0)

    def greet_span(j, _):
        greet((below, j))
        greet((above, j))
        return 0

    lax.fori_loop(0, 16, greet_span, 0)
    for d in range(1, 4):
        greet((lax.rem(z + d, 4) * 2 + c, tl))

    lam = iota((BLK, 128), 0)
    chan = iota((BLK, 128), 1)
    same = (lax.div(lax.rem(lam, 96), 3) == lax.div(chan, 3)) & (chan < 96)
    gmat[...] = jnp.where(same, 1.0, 0.0)
    emat[...] = jnp.where(
        lax.rem(iota((128, BLK), 1), 96) == iota((128, BLK), 0), 1.0, 0.0
    )

    pix_cp.wait()
    frame_id = fid[0].astype(F32)
    lane = iota((128, 128), 1)
    low = lane < 64
    spare = lax.rem(lane, 64) >= 60
    lam1 = iota((1, 256), 1)
    q1 = lax.rem(lam1, 64)
    windows = ((0, 128), (0, 256), (128, 256), (128, 320))
    for n in range(4):
        acc = jnp.zeros((256, 256), F32)
        lo, hi = windows[n]
        for k in range(3):
            w1 = q1 - 20 * k
            target = 80 * n + 20 * lax.div(lam1, 64) + w1
            target = jnp.where((w1 >= 0) & (w1 < 20), target, -1)
            for base in range(lo, hi, 128):
                top = min(base + 128, hi)
                pick = jnp.where(iota((top - base, 256), 0) + base == target, 1.0, 0.0)
                acc = acc + jnp.dot(
                    pixv[k, :, base:top], pick.astype(BF16), preferred_element_type=F32
                )
        for pair in range(2):
            upper = acc[0:128, 128 * pair : 128 * pair + 128]
            lower = acc[128:256, 128 * pair : 128 * pair + 128]
            j = 4 * n + 2 * pair
            even = jnp.where(low, upper, pltpu.roll(lower, 64, 1))
            odd = jnp.where(low, pltpu.roll(upper, 64, 1), lower)
            sbuf[j] = jnp.where(spare, frame_id, even).astype(BF16)
            sbuf[j + 1] = jnp.where(spare, frame_id, odd).astype(BF16)

    pl.semaphore_wait(barrier, 15 + 32 + 3)

    def strip_copy(ch, d):
        j = lax.rem(tl + d, 16)
        rows = pl.ds(64 * ch, 64)
        return remote(
            sbuf.at[j, rows], rbuf.at[d, rows], s1s.at[ch, d], s1r.at[ch, d], (tm, j)
        )

    for ch in range(2):

        def send_strip(d, _, ch=ch):
            strip_copy(ch, d).start()
            return 0

        lax.fori_loop(1, 16, send_strip, 0)
    rbuf[0] = sbuf[tl]

    for cp in x_cps:
        cp.wait()

    def fold(v):
        return v.reshape(v.shape[0] // 8, 8, v.shape[1]).sum(axis=0)

    stin[...] = jnp.zeros((8, BLK), F32)
    for f in range(2):

        def stat_step(i, carry, f=f):
            s, ss = carry
            b = lax.div(i, 8)
            r = pl.multiple_of(lax.rem(i, 8) * 32, 32)
            v = xb[f * 5 + b, pl.ds(r, 32), :].astype(F32)
            return s + fold(v), ss + fold(v * v)

        zero = jnp.zeros((8, BLK), F32)
        s, ss = lax.fori_loop(0, 40, stat_step, (zero, zero))
        stin[2 * f : 2 * f + 1, :] = jnp.sum(s, axis=0, keepdims=True)
        stin[2 * f + 1 : 2 * f + 2, :] = jnp.sum(ss, axis=0, keepdims=True)

    def stat_copy(which, d):
        j = lax.rem(tl + d, 16)
        return remote(
            stsend.at[which],
            strecv.at[which, d],
            sts.at[which, d],
            strs.at[which, d],
            (tm, j),
        )

    def stat_send(which):
        red = jnp.dot(stin[...], gmat[...], precision=HIGHEST, preferred_element_type=F32)
        stsend[which] = red
        strecv[which, 0] = red

        def go(d, _):
            stat_copy(which, d).start()
            return 0

        lax.fori_loop(1, 16, go, 0)

    def stat_wait(which):
        def go(d, _):
            stat_copy(which, d).wait_recv()
            return 0

        lax.fori_loop(1, 16, go, 0)
        return jnp.sum(strecv[which], axis=0)

    stat_send(0)

    spread = jnp.where(lax.div(lax.rem(iota((128, 16), 0), 64), 4) == iota((128, 16), 1), 1.0, 0.0)
    iwr = jnp.dot(spread.astype(BF16), iw[...], preferred_element_type=F32).astype(BF16)
    cw_cp.wait()

    def reduce_tap(k, _):
        gred[k] = lax.dot_general(
            cwv[k], iwr, (((1,), (1,)), ((), ())), preferred_element_type=F32
        )
        return 0

    lax.fori_loop(0, 27, reduce_tap, 0)

    ln = iota((16, 128), 1)
    main = ln < 64
    b0 = lax.rem(ln, 2) == 0
    a0 = lax.rem(lax.div(ln, 2), 2) == 0

    def combine(mc, _):
        r = pl.multiple_of(mc * 16, 16)
        for dt in range(3):
            cols = []
            for dh in range(3):
                g = [gred[9 * dt + 3 * dh + dw, pl.ds(r, 16), :] for dw in range(3)]
                g01 = g[0] + g[1]
                g12 = g[1] + g[2]
                zero = jnp.zeros_like(g01)
                cols.append(
                    (
                        jnp.where(main, jnp.where(b0, g12, zero), jnp.where(b0, zero, g[0])),
                        jnp.where(main, jnp.where(b0, g01, g[2]), zero),
                        jnp.where(main, jnp.where(b0, g[0], g12), zero),
                        jnp.where(main, jnp.where(b0, zero, g01), jnp.where(b0, g[2], zero)),
                    )
                )
            for w in range(4):
                h0, h1, h2 = (cols[dh][w] for dh in range(3))
                h01 = h0 + h1
                h12 = h1 + h2
                zero = jnp.zeros_like(h01)
                taps = (
                    jnp.where(a0, h2, zero),
                    jnp.where(a0, h12, zero),
                    jnp.where(a0, h01, h2),
                    jnp.where(a0, h0, h12),
                    jnp.where(a0, zero, h01),
                    jnp.where(a0, zero, h0),
                )
                for t in range(6):
                    row = pl.multiple_of(t * BLK + w * 96 + r, 16)
                    top = taps[t].astype(BF16)
                    rest = (taps[t] - top.astype(F32)).astype(BF16)
                    bmat[pl.ds(row, 16), 128 * dt : 128 * dt + 128] = top
                    bmat[pl.ds(row, 16), BLK + 128 * dt : BLK + 128 * dt + 128] = rest
        return 0

    lax.fori_loop(0, 6, combine, 0)

    owe = lax.dot_general(
        ow[...].astype(F32), emat[0:96, :], (((0,), (0,)), ((), ())), preferred_element_type=F32
    )
    q = iota((64, BLK), 0)
    kq = lax.div(q, 20)
    wq = lax.rem(q, 20)
    wl = lax.div(iota((64, BLK), 1), 96)
    small = jnp.where(
        kq == 0, owe[0:1, :], jnp.where(kq == 1, owe[1:2, :], jnp.where(kq == 2, owe[2:3, :], 0.0))
    )
    none = jnp.zeros((64, BLK), BF16)
    for b in range(5):
        core = jnp.where(wq == wl + 4 * b, small, 0.0).astype(BF16)
        for half in range(2):
            for copy in range(2):
                at = 128 * copy
                rmat[half, b, at + 64 * half : at + 64 * half + 64, :] = core
                at = at + 64 * (1 - half)
                rmat[half, b, at : at + 64, :] = none

    tot = stat_wait(0) / COUNT
    rows = []
    for f in range(2):
        mean = tot[2 * f : 2 * f + 1]
        meansq = tot[2 * f + 1 : 2 * f + 2]
        rstd = lax.rsqrt(meansq - mean * mean + EPS)
        rows.append((mean, rstd))
    gn = gain[...]
    hb = 0.5 * bias[...]
    table = jnp.concatenate(
        [
            rows[0][0],
            rows[1][0],
            rows[0][1],
            rows[1][1],
            gn,
            hb,
            0.5 * rows[0][1] * gn,
            0.5 * rows[1][1] * gn,
        ],
        axis=0,
    )
    cst[...] = jnp.dot(table, emat[...], precision=HIGHEST, preferred_element_type=F32)

    for f in range(2):
        mean_l = cst[f : f + 1, :]
        a_l = cst[6 + f : 7 + f, :]
        hb_l = cst[5:6, :]
        g2_l = 0.5 * cst[4:5, :]

        def factor_step(i, _, f=f, mean_l=mean_l, a_l=a_l, hb_l=hb_l, g2_l=g2_l):
            b = lax.div(i, 8)
            r = pl.multiple_of(lax.rem(i, 8) * 32, 32)
            v = xb[f * 5 + b, pl.ds(r, 32), :].astype(F32) - mean_l
            u = v * a_l + hb_l
            h = jnp.tanh(u)
            w = (1.0 + u * (1.0 - h)) * ((1.0 + h) * g2_l)
            for i in range(3):
                xs[f * 5 + b, i, pl.ds(r, 32), :] = v[:, 128 * i : 128 * i + 128]
                fs[f * 5 + b, i, pl.ds(r, 32), :] = w[:, 128 * i : 128 * i + 128]
            return 0

        lax.fori_loop(0, 40, factor_step, 0)

    def core_copy(ch):
        return remote(
            sums.at[ch, 1 - c], cbuf.at[ch], cs.at[ch], cr.at[ch], (tm + 1 - 2 * c, tl)
        )

    def z_copy(ch, d):
        zz = lax.rem(z + d, 4)
        return remote(
            part.at[ch, zz],
            zbuf.at[ch, d - 1],
            zs.at[ch, d - 1],
            zr.at[ch, d - 1],
            (zz * 2 + c, tl),
        )

    onehot = None
    for ch in range(2):

        def recv_strip(d, _, ch=ch):
            strip_copy(ch, d).wait_recv()
            return 0

        lax.fori_loop(1, 16, recv_strip, 0)
        if onehot is None:
            ids = rbuf[:, 0:16, :].astype(F32).reshape(256, 128)
            ids = jnp.sum(jnp.where(iota((256, 128), 1) == 60, ids, 0.0), axis=1, keepdims=True)
            at = iota((256, 256), 1)
            order = lax.div(at, 16)
            frame = (
                4 * lax.rem(lax.div(order, 2), 4) + 2 * lax.div(order, 8) + lax.rem(order, 2)
            )
            hit = (ids == frame.astype(F32)) & (
                lax.rem(iota((256, 256), 0), 16) == lax.rem(at, 16)
            )
            onehot = jnp.where(hit, 1.0, 0.0).T.astype(BF16)
        stack = jnp.concatenate(
            [
                rbuf[:, 64 * ch + 16 * g : 64 * ch + 16 * g + 16, :].reshape(256, 128)
                for g in range(4)
            ],
            axis=1,
        )
        total = jnp.dot(onehot, stack, preferred_element_type=F32)
        for g in range(4):
            sums[ch, :, :, :, 16 * g : 16 * g + 16, :] = total[
                :, 128 * g : 128 * g + 128
            ].reshape(2, 4, 2, 16, 128)
        core_copy(ch).start()

    for ch in range(2):
        core_copy(ch).wait_recv()
        part[ch] = sums[ch, c] + cbuf[ch]
        for d in range(1, 4):
            z_copy(ch, d).start()

    for ch in range(2):
        for d in range(1, 4):
            z_copy(ch, d).wait_recv()
        dp = part[ch, z] + (zbuf[ch, 0] + zbuf[ch, 1] + zbuf[ch, 2])
        top = dp.astype(BF16)
        rest = (dp - top.astype(F32)).astype(BF16)
        for f in range(2):
            dpx[128 * f + 64 * ch : 128 * f + 64 * ch + 64, 0:128] = top[f]
            dpx[128 * f + 64 * ch : 128 * f + 64 * ch + 64, 128:256] = rest[f]

    carry = tuple(jnp.zeros((8, 128), F32) for _ in range(12))
    for half in range(2):

        def dxh_step(b, carry, half=half):
            da = jnp.dot(dpx[...], rmat[half, b], preferred_element_type=F32)
            new = []
            for f in range(2):
                at = pl.ds(128 * half, 128)
                s, sx = [], []
                for i in range(3):
                    v = da[128 * f : 128 * f + 128, 128 * i : 128 * i + 128]
                    v = v * fs[f * 5 + b, i, at, :]
                    fs[f * 5 + b, i, at, :] = v
                    s.append(carry[6 * f + i] + fold(v))
                    sx.append(carry[6 * f + 3 + i] + fold(v * xs[f * 5 + b, i, at, :]))
                new += s + sx
            return tuple(new)

        carry = lax.fori_loop(0, 5, dxh_step, carry)
    for i in range(12):
        stin[i // 3 : i // 3 + 1, 128 * (i % 3) : 128 * (i % 3) + 128] = jnp.sum(
            carry[i], axis=0, keepdims=True
        )
    stat_send(1)
    tot = stat_wait(1) / COUNT
    table = []
    for f in range(2):
        rstd = rows[f][1]
        first = tot[2 * f : 2 * f + 1]
        second = tot[2 * f + 1 : 2 * f + 2] * rstd
        table += [rstd, -rstd * rstd * second, -rstd * first, jnp.zeros_like(rstd)]
    cst[...] = jnp.dot(
        jnp.concatenate(table, axis=0), emat[...], precision=HIGHEST, preferred_element_type=F32
    )

    for f in range(2):
        p_l = cst[4 * f : 4 * f + 1, :]
        q_l = cst[4 * f + 1 : 4 * f + 2, :]
        r_l = cst[4 * f + 2 : 4 * f + 3, :]

        def lhs_step(b, _, f=f, p_l=p_l, q_l=q_l, r_l=r_l):
            fb = f * 5 + b
            row = iota((64, 128), 0)
            for rho in range(4):
                sel = pl.ds(rho, 64, stride=4)
                for i in range(3):
                    ls = slice(128 * i, 128 * i + 128)
                    d = p_l[:, ls] * fs[fb, i, sel, :] + q_l[:, ls] * xs[fb, i, sel, :] + r_l[:, ls]
                    at = BLK * (rho + 1) + 128 * i
                    lhs[fb, :, at : at + 128] = d.astype(BF16)
                    if rho == 0:
                        d = jnp.where(row == 63, 0.0, pltpu.roll(d, 63, 0))
                        lhs[fb, :, BLK * 5 + 128 * i : BLK * 5 + 128 * i + 128] = d.astype(BF16)
                    if rho == 3:
                        d = jnp.where(row == 0, 0.0, pltpu.roll(d, 1, 0))
                        lhs[fb, :, 128 * i : 128 * i + 128] = d.astype(BF16)
            return 0

        lax.fori_loop(0, 5, lhs_step, 0)

    left = lhs[...].reshape(640, 6 * BLK)
    ys[...] = jnp.dot(left, bmat[...], preferred_element_type=F32)

    ln = iota((64, 128), 1)
    lo64 = ln < 64
    odd = lax.rem(ln, 2) == 1

    def taken(f, dt, b):
        r = 64 * (5 * f + b)
        return (
            ys[r : r + 64, 128 * dt : 128 * dt + 128]
            + ys[r : r + 64, BLK + 128 * dt : BLK + 128 * dt + 128]
        )

    plans = (
        (1, 0, ((0, 0),)),
        (1, 1, ((0, 1), (1, 0))),
        (0, 0, ((0, 2), (1, 1))),
        (0, 1, ((1, 2),)),
    )
    for group, t, terms in plans:
        cc = []
        for b in range(5):
            v = taken(*terms[0], b)
            for term in terms[1:]:
                v = v + taken(*term, b)
            cc.append(v)
        r1 = pltpu.roll(cc[1], 64, 1)
        r3 = pltpu.roll(cc[3], 64, 1)
        v0 = jnp.where(
            lo64, cc[0] + jnp.where(odd, r1, 0.0), r1 + jnp.where(odd, cc[2], cc[0])
        )
        v1 = jnp.where(
            lo64, cc[2] + jnp.where(odd, r3, r1), r3 + jnp.where(odd, cc[4], cc[2])
        )
        v2 = jnp.where(lo64, cc[4] + jnp.where(odd, 0.0, r3), jnp.where(odd, cc[0], cc[4]))
        for i, v in enumerate((v0, v1, v2)):
            tok[group, 8 * t : 8 * t + 8, :, 128 * i : 128 * i + 128] = v.reshape(8, 8, 128)

    def own_copy(d, sending):
        j = lax.rem(tl + d, 16)
        at = tl if sending else lax.rem(tl + 16 - d, 16)
        return remote(tok.at[0, j], trecv.at[0, at], tks.at[0, d], tkr.at[0, at], (tm, j))

    def span_copy(j, sending):
        at = tl if sending else j
        return remote(tok.at[1, j], trecv.at[1, at], tks.at[1, j], tkr.at[1, at], (below, j))

    def send_span(j, _):
        span_copy(j, True).start()
        return 0

    lax.fori_loop(0, 16, send_span, 0)

    def send_own(d, _):
        own_copy(d, True).start()
        return 0

    lax.fori_loop(1, 16, send_own, 0)
    trecv[0, tl] = tok[0, tl]

    def recv_span(j, _):
        span_copy(j, False).wait_recv()
        return 0

    lax.fori_loop(0, 16, recv_span, 0)

    def recv_own(d, _):
        own_copy(d, False).wait_recv()
        return 0

    lax.fori_loop(1, 16, recv_own, 0)

    ln = iota((8, 128), 1)
    lo8 = ln < 64
    odd8 = lax.rem(ln, 2) == 1
    strips = []
    for j in range(16):
        strips.append(
            [
                trecv[0, j, :, 128 * i : 128 * i + 128]
                + jnp.where(tm < 7, trecv[1, j, :, 128 * i : 128 * i + 128], 0.0)
                for i in range(3)
            ]
        )
    halo = [pltpu.roll(s[2], 64, 1) for s in strips]
    for j in range(16):
        if j > 0:
            strips[j][0] = strips[j][0] + jnp.where(lo8 & ~odd8, halo[j - 1], 0.0)
    done = []
    for j in range(16):
        v2 = strips[j][2]
        if j < 15:
            v2 = v2 + jnp.where(odd8, halo[j + 1], 0.0)
        done.append((strips[j][0], strips[j][1], v2))
    for pair in range(8):
        e = done[2 * pair]
        o = [pltpu.roll(v, 64, 1) for v in done[2 * pair + 1]]
        at = 640 * pair
        out[:, at : at + 128] = e[0]
        out[:, at + 128 : at + 256] = e[1]
        out[:, at + 256 : at + 384] = jnp.where(lo8, e[2], o[0])
        out[:, at + 384 : at + 512] = jnp.where(lo8, o[0], o[1])
        out[:, at + 512 : at + 640] = jnp.where(lo8, o[1], o[2])

    for ch in range(2):

        def sent_strip(d, _, ch=ch):
            strip_copy(ch, d).wait_send()
            stat_copy(ch, d).wait_send()
            return 0

        lax.fori_loop(1, 16, sent_strip, 0)
        core_copy(ch).wait_send()
        for d in range(1, 4):
            z_copy(ch, d).wait_send()

    def sent_own(d, _):
        own_copy(d, True).wait_send()
        return 0

    lax.fori_loop(1, 16, sent_own, 0)

    def sent_span(j, _):
        span_copy(j, True).wait_send()
        return 0

    lax.fori_loop(0, 16, sent_span, 0)


def body(pix_grad, frame_ids, pre_norm, gain, bias, out_weight, conv_weight, in_weight):
    vmem = pl.BlockSpec(memory_space=pltpu.VMEM)
    anyspace = pl.BlockSpec(memory_space=pl.ANY)
    smem = pl.BlockSpec(memory_space=pltpu.SMEM)
    dma = pltpu.SemaphoreType.DMA
    gain = jnp.pad(gain, (0, 32)).reshape(1, 128)
    bias = jnp.pad(bias, (0, 32)).reshape(1, 128)
    return pl.pallas_call(
        kernel,
        out_shape=jax.ShapeDtypeStruct((8, 5120), F32),
        in_specs=[anyspace, smem, anyspace, vmem, vmem, vmem, anyspace, vmem],
        out_specs=vmem,
        scratch_shapes=[
            pltpu.VMEM((3, 256, 320), BF16),
            pltpu.VMEM((PIECES, 256, BLK), BF16),
            pltpu.VMEM((27, 96, 384), BF16),
            pltpu.VMEM((16, 128, 128), BF16),
            pltpu.VMEM((16, 128, 128), BF16),
            pltpu.VMEM((2, 2, 4, 2, 64, 128), F32),
            pltpu.VMEM((2, 4, 2, 64, 128), F32),
            pltpu.VMEM((2, 4, 2, 64, 128), F32),
            pltpu.VMEM((2, 3, 2, 64, 128), F32),
            pltpu.VMEM((256, 256), BF16),
            pltpu.VMEM((2, 5, 256, BLK), BF16),
            pltpu.VMEM((PIECES, 3, 256, 128), F32),
            pltpu.VMEM((PIECES, 3, 256, 128), F32),
            pltpu.VMEM((BLK, 128), F32),
            pltpu.VMEM((128, BLK), F32),
            pltpu.VMEM((8, BLK), F32),
            pltpu.VMEM((2, 8, 128), F32),
            pltpu.VMEM((2, 16, 8, 128), F32),
            pltpu.VMEM((8, BLK), F32),
            pltpu.VMEM((27, 96, 128), F32),
            pltpu.VMEM((6 * BLK, 2 * BLK), BF16),
            pltpu.VMEM((PIECES, 64, 6 * BLK), BF16),
            pltpu.VMEM((640, 2 * BLK), F32),
            pltpu.VMEM((2, 16, 8, BLK), F32),
            pltpu.VMEM((2, 16, 8, BLK), F32),
            dma,
            dma((PIECES,)),
            dma,
            dma((2, 16)),
            dma((2, 16)),
            dma((2,)),
            dma((2,)),
            dma((2, 3)),
            dma((2, 3)),
            dma((2, 16)),
            dma((2, 16)),
            dma((2, 16)),
            dma((2, 16)),
        ],
        compiler_params=pltpu.CompilerParams(
            collective_id=0, has_side_effects=True, vmem_limit_bytes=52 * 1024 * 1024
        ),
    )(pix_grad, frame_ids, pre_norm, gain, bias, out_weight, conv_weight, in_weight)


def solution(mesh):
    return jax.shard_map(
        body,
        mesh=mesh,
        in_specs=(
            P(("tm", "tile"), None, None, None),
            P(("tm", "tile")),
            P("tm", None, "tile"),
            P(),
            P(),
            P(),
            P(),
            P(),
        ),
        out_specs=P(("tm", "tile"), None),
        check_vma=False,
    )
```

time: 614 us -> 56.6 us (0.09); the launches traced: 603 us -> 55.5 us
  waiting for transfers between devices: 224 us -> 0 us
  local copies, waits for them, and re-layouts: 197 us -> 4.18 us
  blocking collectives: 75.2 us -> 0 us
  matrix products: 55.5 us -> 0 us
  Pallas kernels: 0 us -> 50.7 us
  other arithmetic: 20.8 us -> 0 us
  starting transfers between devices: 15.4 us -> 0 us
  between operations: 14.8 us -> 0.67 us
    reduce_scatter x1 -> x0, waiting for transfers between devices: 196 us -> none  [body(): lax.psum_scatter(spread, ('tm', 'tile'), scatter_dimension=0, tiled=True)]
    concatenate x2 -> x0, local copies, waits for them, and re-layouts: 136 us -> none  [body(): jnp.concatenate(pieces, axis=-1)]
    psum x2 -> x0, blocking collectives: 65.2 us -> none  [the longest x1 34.2 us: body(): lax.psum((jnp.sum(grouped_input, axis=(1, 2, 4)), jnp.sum(grouped_input *...]
    dot_general x3 -> x0, matrix products: 55.5 us -> none  [the longest x1 44.5 us: body(): jnp.dot(cols, weights, preferred_element_type=jnp.float32)]
    pallas_call x0 -> x1, Pallas kernels: none -> 50.7 us  [body(): pl.pallas_call(kernel, out_shape=jax.ShapeDtypeStruct((8, 5120), F32), in...]
    unnamed x36 -> x5, local copies, waits for them, and re-layouts: 49 us -> 3.5 us
    ppermute x3 -> x0, waiting for transfers between devices: 28.3 us -> none  [the longest x1 24.2 us: passed_along(): return lax.ppermute(shard, axis, pairs)]
    ppermute x3 -> x0, starting transfers between devices: 15.4 us -> none  [the longest x1 12.8 us: passed_along(): return lax.ppermute(shard, axis, pairs)]
  transfers between devices with their start and end apart: 4 -> 0, of which waited for: 4 -> 0; matrix products, arithmetic and copies ran while one was open for 1% -> 0% of each run, Pallas kernels for 0% -> 0%
where the time goes in v1:
time: 56.6 us; the launch traced here: 55.5 us
  Pallas kernels  50.7 us (90%)
  local copies, waits for them, and re-layouts  4.18 us (7%)
  between operations  0.67 us (1%)
    pallas_call x1, Pallas kernels, body(): pl.pallas_call(kernel, out_shape=jax.ShapeDtypeStruct((8, 5120), F32), in...  50.7 us
    unnamed x5, local copies, waits for them, and re-layouts  3.5 us

profile of v1, /device:TPU:1, one launch (start us, length us, event | category | flops | bytes accessed | tf_op | source)
XLA Modules:
  0.0 55.5 jit_solution(14182798251117659471)
XLA Ops:
  0.7 0.7 %pad_bitcast_fusion = (f32[1,128]{1,0:T(1,128)S(1)}, f32[1,128]{1,0:T(1,128)S(1)}) fusion(f32[96]{0:T(128)} %param.12, f32[96]{0:T(128)} %param.11), kind=kLoop, calls=%fused_computation | loop fusion | bytes 1792 | tf_op jit(solution)/shard_map/reshape | solution.py:615
  1.3 0.8 %copy.10.ow = bf16[96,3]{1,0:T(8,128)(2,1)S(1)} copy(bf16[96,3]{0,1:T(4,128)(2,1)} %param.13) | data formatting | bytes 1152 | tf_op args[5]
  2.1 1.3 %copy.9.pix_hbm = bf16[1,3,256,320]{3,2,1,0:T(8,128)(2,1)S(1)} copy(bf16[1,3,256,320]{2,3,1,0:T(8,128)(2,1)} %param.8) | data formatting | bytes 983040 | tf_op args[0]
  3.5 0.0 copy-start
  3.5 0.7 %copy-done = bf16[16,384]{1,0:T(8,128)(2,1)S(1)} copy-done((bf16[16,384]{1,0:T(8,128)(2,1)S(1)}, bf16[16,384]{1,0:T(8,128)(2,1)}, u32[]{:S(2)}) %copy-start) | copy-done | bytes 12312
  4.2 50.7 %shard_map.82 = f32[8,5120]{1,0:T(8,128)S(1)} custom-call(bf16[1,3,256,320]{3,2,1,0:T(8,128)(2,1)S(1)} %copy.9.pix_hbm, s32[1]{0:T(128)S(6)} %copy.12.fid, bf16[2,256,1920]{2,1,0:T(8,128)(2,1)} %x_hbm.1, f32[1,128]{1,0:T(1,128)S(1)} %get-tuple-element.6.gain, f32[1,128]{1,0:T(1,128)S(1)} %get-tuple-element.5.bias, bf16[96,3]{1,0:T(8,128)(2,1)S(1)} %copy.10.ow, ...), custom_call_target="tpu_custom_call" | custom-call | tf_op jit(solution)/shard_map/pallas_call | solution.py:616
  54.8 0.7 %copy.13 = f32[8,5120]{1,0:T(8,128)} copy(f32[8,5120]{1,0:T(8,128)S(1)} %shard_map.82) | data formatting | bytes 327680
Async XLA Ops:
  3.5 0.7 %copy-start = (bf16[16,384]{1,0:T(8,128)(2,1)S(1)}, bf16[16,384]{1,0:T(8,128)(2,1)}, u32[]{:S(2)}) copy-start(bf16[16,384]{1,0:T(8,128)(2,1)} %iw.1) | copy-start | bytes 36868

commit v2 on v1

v2 whole, which is shorter than its diff:
```python
import functools

import jax
import jax.numpy as jnp
from jax import lax
from jax.experimental import pallas as pl
from jax.experimental.pallas import tpu as pltpu
from jax.sharding import PartitionSpec as P

MESH = pl.DeviceIdType.MESH
F32 = jnp.float32
BF16 = jnp.bfloat16
HIGHEST = lax.Precision.HIGHEST
COUNT = 256.0 * 320.0 * 3.0
EPS = 1e-05
BLK = 384
PIECES = 10


def iota(shape, dim):
    return lax.broadcasted_iota(jnp.int32, shape, dim)


def remote(src, dst, send_sem, recv_sem, device):
    return pltpu.make_async_remote_copy(
        src_ref=src,
        dst_ref=dst,
        send_sem=send_sem,
        recv_sem=recv_sem,
        device_id=device,
        device_id_type=MESH,
    )


def kernel(
    pix_hbm,
    fid,
    x_hbm,
    gain_hbm,
    bias_hbm,
    ow_hbm,
    cw_hbm,
    iw_hbm,
    out,
    gain,
    bias,
    ow,
    iw,
    pixv,
    xb,
    cwv,
    sbuf,
    rbuf,
    picks,
    sums,
    cbuf,
    part,
    zbuf,
    dpx,
    rmat,
    xs,
    fs,
    gmat,
    emat,
    stin,
    stsend,
    strecv,
    table,
    cst,
    gred,
    bmat,
    lhs,
    ys,
    tok,
    trecv,
    pix_sem,
    x_sem,
    cw_sem,
    small_sem,
    s1s,
    s1r,
    cs,
    cr,
    zs,
    zr,
    sts,
    strs,
    tks,
    tkr,
):
    tm = lax.axis_index("tm")
    tl = lax.axis_index("tile")
    z = lax.div(tm, 2)
    c = lax.rem(tm, 2)
    below = lax.rem(tm + 7, 8)
    above = lax.rem(tm + 1, 8)

    pix_cp = pltpu.make_async_copy(pix_hbm.at[0], pixv, pix_sem)
    pix_cp.start()
    x_cps = []
    for f in range(2):
        for b in range(5):
            cp = pltpu.make_async_copy(
                x_hbm.at[f, :, pl.ds(BLK * b, BLK)], xb.at[f * 5 + b], x_sem.at[f * 5 + b]
            )
            cp.start()
            x_cps.append(cp)
    small_cps = []
    for i, (src, dst) in enumerate(
        ((gain_hbm, gain), (bias_hbm, bias), (ow_hbm, ow), (iw_hbm, iw))
    ):
        cp = pltpu.make_async_copy(src, dst, small_sem.at[i])
        cp.start()
        small_cps.append(cp)
    cw_cp = pltpu.make_async_copy(cw_hbm, cwv, cw_sem)
    cw_cp.start()

    barrier = pltpu.get_barrier_semaphore()

    def greet(device):
        pl.semaphore_signal(barrier, inc=1, device_id=device, device_id_type=MESH)

    def greet_tile(d, _):
        j = lax.rem(tl + d, 16)
        greet((tm, j))
        return 0

    lax.fori_loop(1, 16, greet_tile, 0)

    def greet_span(j, _):
        greet((below, j))
        greet((above, j))
        return 0

    lax.fori_loop(0, 16, greet_span, 0)
    for d in range(1, 4):
        greet((lax.rem(z + d, 4) * 2 + c, tl))

    lam = iota((BLK, 128), 0)
    chan = iota((BLK, 128), 1)
    same = (lax.div(lax.rem(lam, 96), 3) == lax.div(chan, 3)) & (chan < 96)
    gmat[...] = jnp.where(same, 1.0, 0.0)
    emat[...] = jnp.where(
        lax.rem(iota((128, BLK), 1), 96) == iota((128, BLK), 0), 1.0, 0.0
    )

    def pack():
        pix_cp.wait()
        frame_id = fid[0].astype(F32)
        r = iota((256, 240), 0)
        m = iota((256, 240), 1)
        slot = lax.rem(r, 64)
        col = 20 * lax.div(r, 64) + lax.rem(slot, 20)
        hit = (slot < 60) & (m == 80 * lax.div(slot, 20) + col)
        pick = jnp.where(hit, 1.0, 0.0).astype(BF16)
        spare = lax.rem(iota((256, 256), 0), 64) >= 60
        for n in range(4):
            stack = jnp.concatenate(
                [pixv[k, 80 * n : 80 * n + 80, :] for k in range(3)], axis=0
            )
            rows = jnp.dot(pick, stack, preferred_element_type=F32)
            rows = jnp.where(spare, frame_id, rows).astype(BF16)
            for jj in range(4):
                for ch in range(2):
                    sbuf[ch, 4 * n + jj] = rows[
                        64 * jj : 64 * jj + 64, 128 * ch : 128 * ch + 128
                    ]

    pack()
    pl.semaphore_wait(barrier, 15 + 32 + 3)

    def strip_copy(ch, d):
        j = lax.rem(tl + d, 16)
        return remote(
            sbuf.at[ch, j], rbuf.at[ch, d], s1s.at[ch, d], s1r.at[ch, d], (tm, j)
        )

    for ch in range(2):

        def send_strip(d, _, ch=ch):
            strip_copy(ch, d).start()
            return 0

        lax.fori_loop(1, 16, send_strip, 0)
    for ch in range(2):
        rbuf[ch, 0] = sbuf[ch, tl]

    for cp in x_cps:
        cp.wait()

    def fold(v):
        return v.reshape(v.shape[0] // 8, 8, v.shape[1]).sum(axis=0)

    def stats():
        stin[...] = jnp.zeros((8, BLK), F32)
        for f in range(2):

            def stat_step(i, carry, f=f):
                s, ss = carry
                b = lax.div(i, 8)
                r = pl.multiple_of(lax.rem(i, 8) * 32, 32)
                v = xb[f * 5 + b, pl.ds(r, 32), :].astype(F32)
                return s + fold(v), ss + fold(v * v)

            zero = jnp.zeros((8, BLK), F32)
            s, ss = lax.fori_loop(0, 40, stat_step, (zero, zero))
            stin[2 * f : 2 * f + 1, :] = jnp.sum(s, axis=0, keepdims=True)
            stin[2 * f + 1 : 2 * f + 2, :] = jnp.sum(ss, axis=0, keepdims=True)

    stats()

    def stat_copy(which, d):
        j = lax.rem(tl + d, 16)
        return remote(
            stsend.at[which],
            strecv.at[which, d],
            sts.at[which, d],
            strs.at[which, d],
            (tm, j),
        )

    def stat_send(which):
        red = jnp.dot(stin[...], gmat[...], precision=HIGHEST, preferred_element_type=F32)
        stsend[which] = red
        strecv[which, 0] = red

        def go(d, _):
            stat_copy(which, d).start()
            return 0

        lax.fori_loop(1, 16, go, 0)

    def stat_wait(which):
        def go(d, _):
            stat_copy(which, d).wait_recv()
            return 0

        lax.fori_loop(1, 16, go, 0)
        return jnp.sum(strecv[which], axis=0)

    stat_send(0)

    cw_cp.wait()
    for cp in small_cps:
        cp.wait()

    spread = jnp.where(lax.div(lax.rem(iota((128, 16), 0), 64), 4) == iota((128, 16), 1), 1.0, 0.0)
    iwr = jnp.dot(spread.astype(BF16), iw[...], preferred_element_type=F32).astype(BF16)

    def reduce_tap(k, _):
        gred[k] = lax.dot_general(
            cwv[k], iwr, (((1,), (1,)), ((), ())), preferred_element_type=F32
        )
        return 0

    def taps_reduced():
        lax.fori_loop(0, 27, reduce_tap, 0)

    taps_reduced()

    ln = iota((16, 128), 1)
    main = ln < 64
    b0 = lax.rem(ln, 2) == 0
    a0 = lax.rem(lax.div(ln, 2), 2) == 0

    def combine(mc, _):
        r = pl.multiple_of(mc * 16, 16)
        for dt in range(3):
            cols = []
            for dh in range(3):
                g = [gred[9 * dt + 3 * dh + dw, pl.ds(r, 16), :] for dw in range(3)]
                g01 = g[0] + g[1]
                g12 = g[1] + g[2]
                zero = jnp.zeros_like(g01)
                cols.append(
                    (
                        jnp.where(main, jnp.where(b0, g12, zero), jnp.where(b0, zero, g[0])),
                        jnp.where(main, jnp.where(b0, g01, g[2]), zero),
                        jnp.where(main, jnp.where(b0, g[0], g12), zero),
                        jnp.where(main, jnp.where(b0, zero, g01), jnp.where(b0, g[2], zero)),
                    )
                )
            for w in range(4):
                h0, h1, h2 = (cols[dh][w] for dh in range(3))
                h01 = h0 + h1
                h12 = h1 + h2
                zero = jnp.zeros_like(h01)
                taps = (
                    jnp.where(a0, h2, zero),
                    jnp.where(a0, h12, zero),
                    jnp.where(a0, h01, h2),
                    jnp.where(a0, h0, h12),
                    jnp.where(a0, zero, h01),
                    jnp.where(a0, zero, h0),
                )
                for t in range(6):
                    row = pl.multiple_of(t * BLK + w * 96 + r, 16)
                    top = taps[t].astype(BF16)
                    rest = (taps[t] - top.astype(F32)).astype(BF16)
                    bmat[pl.ds(row, 16), 128 * dt : 128 * dt + 128] = top
                    bmat[pl.ds(row, 16), BLK + 128 * dt : BLK + 128 * dt + 128] = rest
        return 0

    def weights():
        lax.fori_loop(0, 6, combine, 0)

    weights()

    def colours():
        owe = jnp.dot(ow[...].astype(F32), emat[0:96, :], preferred_element_type=F32)
        q = iota((64, BLK), 0)
        kq = lax.div(q, 20)
        wq = lax.rem(q, 20)
        wl = lax.div(iota((64, BLK), 1), 96)
        small = jnp.where(
            kq == 0,
            owe[0:1, :],
            jnp.where(kq == 1, owe[1:2, :], jnp.where(kq == 2, owe[2:3, :], 0.0)),
        )
        for b in range(5):
            core = jnp.where(wq == wl + 4 * b, small, 0.0).astype(BF16)
            rmat[b, 0:64, :] = core
            rmat[b, 64:128, :] = core

    colours()

    tot = stat_wait(0) / COUNT
    rows = []
    for f in range(2):
        mean = tot[2 * f : 2 * f + 1]
        meansq = tot[2 * f + 1 : 2 * f + 2]
        rstd = lax.rsqrt(meansq - mean * mean + EPS)
        rows.append((mean, rstd))
    table[...] = jnp.zeros((8, 128), F32)
    for f in range(2):
        table[f : f + 1, :] = rows[f][0]
        table[6 + f : 7 + f, 0:96] = 0.5 * rows[f][1][:, 0:96] * gain[...]
    table[4:5, 0:96] = gain[...]
    table[5:6, 0:96] = 0.5 * bias[...]
    cst[...] = jnp.dot(table[...], emat[...], precision=HIGHEST, preferred_element_type=F32)

    def factor():
        for f in range(2):
            mean_l = cst[f : f + 1, :]
            a_l = cst[6 + f : 7 + f, :]
            hb_l = cst[5:6, :]
            g2_l = 0.5 * cst[4:5, :]

            def factor_step(i, _, f=f, mean_l=mean_l, a_l=a_l, hb_l=hb_l, g2_l=g2_l):
                b = lax.div(i, 8)
                r = pl.multiple_of(lax.rem(i, 8) * 32, 32)
                v = xb[f * 5 + b, pl.ds(r, 32), :].astype(F32) - mean_l
                u = v * a_l + hb_l
                h = jnp.tanh(u)
                w = (1.0 + u * (1.0 - h)) * ((1.0 + h) * g2_l)
                for i in range(3):
                    xs[f * 5 + b, i, pl.ds(r, 32), :] = v[:, 128 * i : 128 * i + 128]
                    fs[f * 5 + b, i, pl.ds(r, 32), :] = w[:, 128 * i : 128 * i + 128]
                return 0

            lax.fori_loop(0, 40, factor_step, 0)

    factor()

    def core_copy(ch):
        return remote(
            sums.at[ch, 1 - c], cbuf.at[ch], cs.at[ch], cr.at[ch], (tm + 1 - 2 * c, tl)
        )

    def z_copy(ch, d):
        zz = lax.rem(z + d, 4)
        return remote(
            part.at[ch, zz],
            zbuf.at[ch, d - 1],
            zs.at[ch, d - 1],
            zr.at[ch, d - 1],
            (zz * 2 + c, tl),
        )

    def frame_picks():
        ids = rbuf[0, :, 48:64, :].astype(F32)
        ids = jnp.broadcast_to(ids[:, 15:16, :], (16, 16, 128)).reshape(256, 128)
        ids = jnp.concatenate([ids, ids], axis=1)
        at = iota((256, 256), 1)
        order = lax.div(at, 16)
        frame = 4 * lax.rem(lax.div(order, 2), 4) + 2 * lax.div(order, 8) + lax.rem(order, 2)
        hit = (ids == frame.astype(F32)) & (lax.rem(iota((256, 256), 0), 16) == lax.rem(at, 16))
        picks[...] = jnp.where(hit, 1.0, 0.0).T.astype(BF16)

    def frame_sums(ch):
        stack = jnp.concatenate(
            [rbuf[ch, :, 16 * g : 16 * g + 16, :].reshape(256, 128) for g in range(4)], axis=1
        )
        total = jnp.dot(picks[...], stack, preferred_element_type=F32)
        for g in range(4):
            sums[ch, :, :, :, 16 * g : 16 * g + 16, :] = total[
                :, 128 * g : 128 * g + 128
            ].reshape(2, 4, 2, 16, 128)

    for ch in range(2):

        def recv_strip(d, _, ch=ch):
            strip_copy(ch, d).wait_recv()
            return 0

        lax.fori_loop(1, 16, recv_strip, 0)
        if ch == 0:
            frame_picks()
        frame_sums(ch)
        core_copy(ch).start()

    for ch in range(2):
        core_copy(ch).wait_recv()
        part[ch] = sums[ch, c] + cbuf[ch]
        for d in range(1, 4):
            z_copy(ch, d).start()

    for ch in range(2):
        for d in range(1, 4):
            z_copy(ch, d).wait_recv()
        def frame_rows(ch=ch):
            dp = part[ch, z] + (zbuf[ch, 0] + zbuf[ch, 1] + zbuf[ch, 2])
            for f in range(2):
                top = dp[f].astype(BF16)
                rest = dp[f] - top.astype(F32)
                both = jnp.concatenate([top.astype(F32), rest], axis=0).T
                dpx[ch, 128 * f : 128 * f + 128, :] = both.astype(BF16)

        frame_rows()

    def dxh():
        carry = tuple(jnp.zeros((8, 128), F32) for _ in range(12))
        for half in range(2):

            def dxh_step(b, carry, half=half):
                da = jnp.dot(dpx[half], rmat[b], preferred_element_type=F32)
                new = []
                for f in range(2):
                    at = pl.ds(128 * half, 128)
                    s, sx = [], []
                    for i in range(3):
                        v = da[128 * f : 128 * f + 128, 128 * i : 128 * i + 128]
                        v = v * fs[f * 5 + b, i, at, :]
                        fs[f * 5 + b, i, at, :] = v
                        s.append(carry[6 * f + i] + fold(v))
                        sx.append(carry[6 * f + 3 + i] + fold(v * xs[f * 5 + b, i, at, :]))
                    new += s + sx
                return tuple(new)

            carry = lax.fori_loop(0, 5, dxh_step, carry)
        for i in range(12):
            stin[i // 3 : i // 3 + 1, 128 * (i % 3) : 128 * (i % 3) + 128] = jnp.sum(
                carry[i], axis=0, keepdims=True
            )

    dxh()
    stat_send(1)
    tot = stat_wait(1) / COUNT
    terms = []
    for f in range(2):
        rstd = rows[f][1]
        first = tot[2 * f : 2 * f + 1]
        second = tot[2 * f + 1 : 2 * f + 2] * rstd
        terms += [rstd, -rstd * rstd * second, -rstd * first, jnp.zeros_like(rstd)]
    cst[...] = jnp.dot(
        jnp.concatenate(terms, axis=0), emat[...], precision=HIGHEST, preferred_element_type=F32
    )

    def left_side():
        for f in range(2):
            p_l = cst[4 * f : 4 * f + 1, :]
            q_l = cst[4 * f + 1 : 4 * f + 2, :]
            r_l = cst[4 * f + 2 : 4 * f + 3, :]

            def lhs_step(b, _, f=f, p_l=p_l, q_l=q_l, r_l=r_l):
                fb = f * 5 + b
                row = iota((64, 128), 0)
                for rho in range(4):
                    sel = pl.ds(rho, 64, stride=4)
                    for i in range(3):
                        ls = slice(128 * i, 128 * i + 128)
                        d = p_l[:, ls] * fs[fb, i, sel, :] + q_l[:, ls] * xs[fb, i, sel, :] + r_l[:, ls]
                        at = BLK * (rho + 1) + 128 * i
                        lhs[fb, :, at : at + 128] = d.astype(BF16)
                        if rho == 0:
                            d = jnp.where(row == 63, 0.0, pltpu.roll(d, 63, 0))
                            lhs[fb, :, BLK * 5 + 128 * i : BLK * 5 + 128 * i + 128] = d.astype(BF16)
                        if rho == 3:
                            d = jnp.where(row == 0, 0.0, pltpu.roll(d, 1, 0))
                            lhs[fb, :, 128 * i : 128 * i + 128] = d.astype(BF16)
                return 0

            lax.fori_loop(0, 5, lhs_step, 0)

    left_side()

    def conv():
        left = lhs[...].reshape(640, 6 * BLK)
        ys[...] = jnp.dot(left, bmat[...], preferred_element_type=F32)

    conv()

    ln = iota((64, 128), 1)
    lo64 = ln < 64
    odd = lax.rem(ln, 2) == 1

    def taken(f, dt, b):
        r = 64 * (5 * f + b)
        return (
            ys[r : r + 64, 128 * dt : 128 * dt + 128]
            + ys[r : r + 64, BLK + 128 * dt : BLK + 128 * dt + 128]
        )

    plans = (
        (1, 0, ((0, 0),)),
        (1, 1, ((0, 1), (1, 0))),
        (0, 0, ((0, 2), (1, 1))),
        (0, 1, ((1, 2),)),
    )
    def tokens():
        for group, t, terms in plans:
            cc = []
            for b in range(5):
                v = taken(*terms[0], b)
                for term in terms[1:]:
                    v = v + taken(*term, b)
                cc.append(v)
            r1 = pltpu.roll(cc[1], 64, 1)
            r3 = pltpu.roll(cc[3], 64, 1)
            v0 = jnp.where(
                lo64, cc[0] + jnp.where(odd, r1, 0.0), r1 + jnp.where(odd, cc[2], cc[0])
            )
            v1 = jnp.where(
                lo64, cc[2] + jnp.where(odd, r3, r1), r3 + jnp.where(odd, cc[4], cc[2])
            )
            v2 = jnp.where(lo64, cc[4] + jnp.where(odd, 0.0, r3), jnp.where(odd, cc[0], cc[4]))
            for i, v in enumerate((v0, v1, v2)):
                tok[group, 8 * t : 8 * t + 8, :, 128 * i : 128 * i + 128] = v.reshape(8, 8, 128)

    tokens()

    def own_copy(d, sending):
        j = lax.rem(tl + d, 16)
        at = tl if sending else lax.rem(tl + 16 - d, 16)
        return remote(tok.at[0, j], trecv.at[0, at], tks.at[0, d], tkr.at[0, at], (tm, j))

    def span_copy(j, sending):
        at = tl if sending else j
        return remote(tok.at[1, j], trecv.at[1, at], tks.at[1, j], tkr.at[1, at], (below, j))

    def send_span(j, _):
        span_copy(j, True).start()
        return 0

    lax.fori_loop(0, 16, send_span, 0)

    def send_own(d, _):
        own_copy(d, True).start()
        return 0

    lax.fori_loop(1, 16, send_own, 0)
    trecv[0, tl] = tok[0, tl]

    def recv_span(j, _):
        span_copy(j, False).wait_recv()
        return 0

    lax.fori_loop(0, 16, recv_span, 0)

    def recv_own(d, _):
        own_copy(d, False).wait_recv()
        return 0

    lax.fori_loop(1, 16, recv_own, 0)

    def assemble():
        ln = iota((8, 128), 1)
        lo8 = ln < 64
        odd8 = lax.rem(ln, 2) == 1
        strips = []
        for j in range(16):
            strips.append(
                [
                    trecv[0, j, :, 128 * i : 128 * i + 128]
                    + jnp.where(tm < 7, trecv[1, j, :, 128 * i : 128 * i + 128], 0.0)
                    for i in range(3)
                ]
            )
        halo = [pltpu.roll(s[2], 64, 1) for s in strips]
        for j in range(16):
            if j > 0:
                strips[j][0] = strips[j][0] + jnp.where(lo8 & ~odd8, halo[j - 1], 0.0)
        done = []
        for j in range(16):
            v2 = strips[j][2]
            if j < 15:
                v2 = v2 + jnp.where(odd8, halo[j + 1], 0.0)
            done.append((strips[j][0], strips[j][1], v2))
        for pair in range(8):
            e = done[2 * pair]
            o = [pltpu.roll(v, 64, 1) for v in done[2 * pair + 1]]
            at = 640 * pair
            out[:, at : at + 128] = e[0]
            out[:, at + 128 : at + 256] = e[1]
            out[:, at + 256 : at + 384] = jnp.where(lo8, e[2], o[0])
            out[:, at + 384 : at + 512] = jnp.where(lo8, o[0], o[1])
            out[:, at + 512 : at + 640] = jnp.where(lo8, o[1], o[2])

    assemble()

    for ch in range(2):

        def sent_strip(d, _, ch=ch):
            strip_copy(ch, d).wait_send()
            stat_copy(ch, d).wait_send()
            return 0

        lax.fori_loop(1, 16, sent_strip, 0)
        core_copy(ch).wait_send()
        for d in range(1, 4):
            z_copy(ch, d).wait_send()

    def sent_own(d, _):
        own_copy(d, True).wait_send()
        return 0

    lax.fori_loop(1, 16, sent_own, 0)

    def sent_span(j, _):
        span_copy(j, True).wait_send()
        return 0

    lax.fori_loop(0, 16, sent_span, 0)


def body(pix_grad, frame_ids, pre_norm, gain, bias, out_weight, conv_weight, in_weight):
    hbm = pl.BlockSpec(memory_space=pltpu.HBM)
    smem = pl.BlockSpec(memory_space=pltpu.SMEM)
    dma = pltpu.SemaphoreType.DMA
    pix_grad = jnp.transpose(pix_grad, (0, 1, 3, 2))
    out_weight = out_weight.T
    gain = gain.reshape(1, 96)
    bias = bias.reshape(1, 96)
    return pl.pallas_call(
        kernel,
        out_shape=jax.ShapeDtypeStruct((8, 5120), F32),
        in_specs=[hbm, smem] + [hbm] * 6,
        out_specs=pl.BlockSpec(memory_space=pltpu.VMEM),
        scratch_shapes=[
            pltpu.VMEM((1, 96), F32),
            pltpu.VMEM((1, 96), F32),
            pltpu.VMEM((3, 96), BF16),
            pltpu.VMEM((16, 384), BF16),
            pltpu.VMEM((3, 320, 256), BF16),
            pltpu.VMEM((PIECES, 256, BLK), BF16),
            pltpu.VMEM((27, 96, 384), BF16),
            pltpu.VMEM((2, 16, 64, 128), BF16),
            pltpu.VMEM((2, 16, 64, 128), BF16),
            pltpu.VMEM((256, 256), BF16),
            pltpu.VMEM((2, 2, 4, 2, 64, 128), F32),
            pltpu.VMEM((2, 4, 2, 64, 128), F32),
            pltpu.VMEM((2, 4, 2, 64, 128), F32),
            pltpu.VMEM((2, 3, 2, 64, 128), F32),
            pltpu.VMEM((2, 256, 128), BF16),
            pltpu.VMEM((5, 128, BLK), BF16),
            pltpu.VMEM((PIECES, 3, 256, 128), F32),
            pltpu.VMEM((PIECES, 3, 256, 128), F32),
            pltpu.VMEM((BLK, 128), F32),
            pltpu.VMEM((128, BLK), F32),
            pltpu.VMEM((8, BLK), F32),
            pltpu.VMEM((2, 8, 128), F32),
            pltpu.VMEM((2, 16, 8, 128), F32),
            pltpu.VMEM((8, 128), F32),
            pltpu.VMEM((8, BLK), F32),
            pltpu.VMEM((27, 96, 128), F32),
            pltpu.VMEM((6 * BLK, 2 * BLK), BF16),
            pltpu.VMEM((PIECES, 64, 6 * BLK), BF16),
            pltpu.VMEM((640, 2 * BLK), F32),
            pltpu.VMEM((2, 16, 8, BLK), F32),
            pltpu.VMEM((2, 16, 8, BLK), F32),
            dma,
            dma((PIECES,)),
            dma,
            dma((4,)),
            dma((2, 16)),
            dma((2, 16)),
            dma((2,)),
            dma((2,)),
            dma((2, 3)),
            dma((2, 3)),
            dma((2, 16)),
            dma((2, 16)),
            dma((2, 16)),
            dma((2, 16)),
        ],
        compiler_params=pltpu.CompilerParams(
            collective_id=0, has_side_effects=True, vmem_limit_bytes=62 * 1024 * 1024
        ),
    )(pix_grad, frame_ids, pre_norm, gain, bias, out_weight, conv_weight, in_weight)


def solution(mesh):
    return jax.shard_map(
        body,
        mesh=mesh,
        in_specs=(
            P(("tm", "tile"), None, None, None),
            P(("tm", "tile")),
            P("tm", None, "tile"),
            P(),
            P(),
            P(),
            P(),
            P(),
        ),
        out_specs=P(("tm", "tile"), None),
        check_vma=False,
    )
```

time: 56.6 us -> 54.5 us (0.963)
  local copies, waits for them, and re-layouts: 4.18 us -> 1.59 us
    unnamed x5 -> x1, local copies, waits for them, and re-layouts: 3.5 us -> 1.59 us
    reshape x1 -> x0, local copies, waits for them, and re-layouts: 0.68 us -> none  [body(): bias = jnp.pad(bias, (0, 32)).reshape(1, 128)]
    pallas_call x1, Pallas kernels: 50.7 us -> 51.2 us  [body(): pl.pallas_call(kernel, out_shape=jax.ShapeDtypeStruct((8, 5120), F32), in...]
where the time goes in v2:
time: 54.5 us; the launch traced here: 53.5 us
  Pallas kernels  51.2 us (94%)
  local copies, waits for them, and re-layouts  1.59 us (3%)
  between operations  0.66 us (1%)
    pallas_call x1, Pallas kernels, body(): pl.pallas_call(kernel, out_shape=jax.ShapeDtypeStruct((8, 5120), F32), in...  51.2 us
    unnamed x1, local copies, waits for them, and re-layouts  1.59 us

profile of v2, /device:TPU:1, one launch (start us, length us, event | category | flops | bytes accessed | tf_op | source)
XLA Modules:
  0.0 53.5 jit_solution(15303448859814140112)
XLA Ops:
  0.7 51.2 %shard_map.82 = f32[8,5120]{1,0:T(8,128)} custom-call(bf16[1,3,320,256]{3,2,1,0:T(8,128)(2,1)} %bitcast.4, s32[1]{0:T(128)S(6)} %copy.10.fid, bf16[2,256,1920]{2,1,0:T(8,128)(2,1)} %x_hbm.1, f32[1,96]{1,0:T(1,128)} %bitcast.6, f32[1,96]{1,0:T(1,128)} %bitcast.7, bf16[3,96]{1,0:T(4,128)(2,1)} %bitcast.5, bf16[27,96,384]{2,1,0:T(8,128)(2,1)} %cw_hbm.1, ...), custom_call_target="tpu_custom_call" | custom-call | tf_op jit(solution)/shard_map/pallas_call | solution.py:644
  51.9 1.6 %copy.11 = f32[8,5120]{1,0:T(8,128)} copy(f32[8,5120]{1,0:T(8,128)} %shard_map.82) | data formatting | bytes 327680

commit v3 on v2

--- a/solution.py
+++ b/solution.py
@@ -1,5 +1,3 @@
-import functools
-
 import jax
 import jax.numpy as jnp
 from jax import lax
@@ -13,6 +11,8 @@
 HIGHEST = lax.Precision.HIGHEST
 COUNT = 256.0 * 320.0 * 3.0
 EPS = 1e-05
+EIGHTHS = 8.0 / 0.6931471805599453
+RANGE = 32700.0
 BLK = 384
 PIECES = 10
 
@@ -53,8 +53,7 @@
     rbuf,
     picks,
     sums,
-    cbuf,
-    part,
+    packs,
     zbuf,
     dpx,
     rmat,
@@ -79,8 +78,6 @@
     small_sem,
     s1s,
     s1r,
-    cs,
-    cr,
     zs,
     zr,
     sts,
@@ -120,21 +117,17 @@
     def greet(device):
         pl.semaphore_signal(barrier, inc=1, device_id=device, device_id_type=MESH)
 
-    def greet_tile(d, _):
+    def greet_chip(d, _):
         j = lax.rem(tl + d, 16)
         greet((tm, j))
-        return 0
-
-    lax.fori_loop(1, 16, greet_tile, 0)
-
-    def greet_span(j, _):
-        greet((below, j))
-        greet((above, j))
-        return 0
-
-    lax.fori_loop(0, 16, greet_span, 0)
+        greet((tm + 1 - 2 * c, j))
+        return 0
+
+    lax.fori_loop(1, 16, greet_chip, 0)
+    greet((tm + 1 - 2 * c, tl))
     for d in range(1, 4):
-        greet((lax.rem(z + d, 4) * 2 + c, tl))
+        for r in range(2):
+            greet((lax.rem(z + d, 4) * 2 + lax.rem(c + r, 2), tl))
 
     lam = iota((BLK, 128), 0)
     chan = iota((BLK, 128), 1)
@@ -145,7 +138,6 @@
     )
 
     def pack():
-        pix_cp.wait()
         frame_id = fid[0].astype(F32)
         r = iota((256, 240), 0)
         m = iota((256, 240), 1)
@@ -166,24 +158,22 @@
                         64 * jj : 64 * jj + 64, 128 * ch : 128 * ch + 128
                     ]
 
+    pix_cp.wait()
     pack()
-    pl.semaphore_wait(barrier, 15 + 32 + 3)
-
-    def strip_copy(ch, d):
+    def strip_copy(r, d):
         j = lax.rem(tl + d, 16)
-        return remote(
-            sbuf.at[ch, j], rbuf.at[ch, d], s1s.at[ch, d], s1r.at[ch, d], (tm, j)
-        )
-
-    for ch in range(2):
-
-        def send_strip(d, _, ch=ch):
-            strip_copy(ch, d).start()
+        h = lax.rem(c + r, 2)
+        return remote(sbuf.at[h, j], rbuf.at[r, d], s1s.at[r, d], s1r.at[r, d], (2 * z + h, j))
+
+    def strips_sent():
+        def send_strip(d, _):
+            strip_copy(0, d).start()
+            strip_copy(1, d).start()
             return 0
 
         lax.fori_loop(1, 16, send_strip, 0)
-    for ch in range(2):
-        rbuf[ch, 0] = sbuf[ch, tl]
+        strip_copy(1, 0).start()
+        rbuf[0, 0] = sbuf[c, tl]
 
     for cp in x_cps:
         cp.wait()
@@ -208,6 +198,8 @@
             stin[2 * f + 1 : 2 * f + 2, :] = jnp.sum(ss, axis=0, keepdims=True)
 
     stats()
+    pl.semaphore_wait(barrier, 31 + 6)
+    strips_sent()
 
     def stat_copy(which, d):
         j = lax.rem(tl + d, 16)
@@ -240,22 +232,132 @@
 
     stat_send(0)
 
-    cw_cp.wait()
+    def colours():
+        owe = jnp.dot(ow[...].astype(F32), emat[0:96, :], preferred_element_type=F32)
+        q = iota((64, BLK), 0)
+        kq = lax.div(q, 20)
+        wq = lax.rem(q, 20)
+        wl = lax.div(iota((64, BLK), 1), 96)
+        small = jnp.where(
+            kq == 0,
+            owe[0:1, :],
+            jnp.where(kq == 1, owe[1:2, :], jnp.where(kq == 2, owe[2:3, :], 0.0)),
+        )
+        for b in range(5):
+            core = jnp.where(wq == wl + 4 * b, small, 0.0).astype(BF16)
+            rmat[b, 0:64, :] = core
+            rmat[b, 64:128, :] = core
+
     for cp in small_cps:
         cp.wait()
+    colours()
+
+    tot = stat_wait(0) / COUNT
+    rows = []
+    for f in range(2):
+        mean = tot[2 * f : 2 * f + 1]
+        meansq = tot[2 * f + 1 : 2 * f + 2]
+        rstd = lax.rsqrt(meansq - mean * mean + EPS)
+        rows.append((mean, rstd))
+    table[...] = jnp.zeros((8, 128), F32)
+    for f in range(2):
+        table[f : f + 1, :] = rows[f][0]
+        table[6 + f : 7 + f, 0:96] = 0.5 * rows[f][1][:, 0:96] * gain[...]
+    table[4:5, 0:96] = gain[...]
+    table[5:6, 0:96] = 0.5 * bias[...]
+    cst[...] = jnp.dot(table[...], emat[...], precision=HIGHEST, preferred_element_type=F32)
+
+    def factor():
+        for f in range(2):
+            mean_l = cst[f : f + 1, :]
+            a_l = cst[6 + f : 7 + f, :]
+            hb_l = cst[5:6, :]
+            g2_l = 0.5 * cst[4:5, :]
+
+            def factor_step(i, _, f=f, mean_l=mean_l, a_l=a_l, hb_l=hb_l, g2_l=g2_l):
+                b = lax.div(i, 8)
+                r = pl.multiple_of(lax.rem(i, 8) * 32, 32)
+                v = xb[f * 5 + b, pl.ds(r, 32), :].astype(F32) - mean_l
+                u = v * a_l + hb_l
+                h = jnp.tanh(u)
+                w = (1.0 + u * (1.0 - h)) * ((1.0 + h) * g2_l)
+                for i in range(3):
+                    xs[f * 5 + b, i, pl.ds(r, 32), :] = v[:, 128 * i : 128 * i + 128]
+                    fs[f * 5 + b, i, pl.ds(r, 32), :] = w[:, 128 * i : 128 * i + 128]
+                return 0
+
+            lax.fori_loop(0, 40, factor_step, 0)
+
+    factor()
+
+    def frame_picks():
+        for r in range(2):
+            ids = rbuf[r, :, 48:64, :].astype(F32)
+            ids = jnp.broadcast_to(ids[:, 15:16, :], (16, 16, 128)).reshape(256, 128)
+            ids = jnp.concatenate([ids, ids], axis=1)
+            at = iota((256, 256), 1)
+            hit = (ids == lax.div(at, 16).astype(F32)) & (
+                lax.rem(iota((256, 256), 0), 16) == lax.rem(at, 16)
+            )
+            picks[:, 256 * r : 256 * r + 256] = jnp.where(hit, 1.0, 0.0).T.astype(BF16)
+
+    def frame_sums():
+        stack = jnp.concatenate(
+            [rbuf[:, :, 16 * g : 16 * g + 16, :].reshape(512, 128) for g in range(4)], axis=1
+        )
+        total = jnp.dot(picks[...], stack, preferred_element_type=F32)
+        for g in range(4):
+            v = total[:, 128 * g : 128 * g + 128].reshape(8, 2, 16, 128)
+            if g == 3:
+                v = jnp.where(iota(v.shape, 2) >= 12, 0.0, v)
+            sums[:, :, 16 * g : 16 * g + 16, :] = v
+
+    def packed():
+        for owner in range(8):
+            v = sums[owner]
+            largest = jnp.max(jnp.maximum(v[0], v[1]), axis=0, keepdims=True)
+            smallest = jnp.min(jnp.minimum(v[0], v[1]), axis=0, keepdims=True)
+            largest = jnp.maximum(jnp.maximum(largest, -smallest), 1e-20)
+            step = jnp.floor(jnp.log(largest) * EIGHTHS) + 2.0
+            scale = RANGE * jnp.exp(step * (-1.0 / EIGHTHS))
+            w = jnp.round(v * scale[None])
+            w = jnp.where(iota(v.shape, 1) >= 60, step[None], w)
+            packs[owner] = w.astype(jnp.int32).astype(jnp.int16)
+
+    def unpacked(v):
+        v = v.astype(jnp.int32).astype(F32)
+        return v * (jnp.exp(v[:, 60:61, :] * (1.0 / EIGHTHS)) * (1.0 / RANGE))
+
+    def z_copy(r, d):
+        owner = lax.rem(z + d, 4) * 2 + lax.rem(c + r, 2)
+        return remote(packs.at[owner], zbuf.at[r, d], zs.at[r, d], zr.at[r, d], (owner, tl))
+
+    partners = tuple((r, d) for r in range(2) for d in range(4) if r + d > 0)
+
+    def recv_strip(d, _):
+        strip_copy(0, d).wait_recv()
+        strip_copy(1, d).wait_recv()
+        return 0
+
+    lax.fori_loop(1, 16, recv_strip, 0)
+    strip_copy(1, 0).wait_recv()
+    frame_picks()
+    frame_sums()
+    packed()
+    for r, d in partners:
+        z_copy(r, d).start()
+
 
     spread = jnp.where(lax.div(lax.rem(iota((128, 16), 0), 64), 4) == iota((128, 16), 1), 1.0, 0.0)
-    iwr = jnp.dot(spread.astype(BF16), iw[...], preferred_element_type=F32).astype(BF16)
-
-    def reduce_tap(k, _):
-        gred[k] = lax.dot_general(
-            cwv[k], iwr, (((1,), (1,)), ((), ())), preferred_element_type=F32
-        )
-        return 0
 
     def taps_reduced():
-        lax.fori_loop(0, 27, reduce_tap, 0)
-
+        iwr = jnp.dot(spread.astype(BF16), iw[...], preferred_element_type=F32).T.astype(BF16)
+        for i in range(9):
+            gred[3 * i : 3 * i + 3] = jnp.dot(
+                cwv[3 * i : 3 * i + 3].reshape(288, BLK), iwr, preferred_element_type=F32
+            ).reshape(3, 96, 128)
+
+    cw_cp.wait()
     taps_reduced()
 
     ln = iota((16, 128), 1)
@@ -306,127 +408,20 @@
 
     weights()
 
-    def colours():
-        owe = jnp.dot(ow[...].astype(F32), emat[0:96, :], preferred_element_type=F32)
-        q = iota((64, BLK), 0)
-        kq = lax.div(q, 20)
-        wq = lax.rem(q, 20)
-        wl = lax.div(iota((64, BLK), 1), 96)
-        small = jnp.where(
-            kq == 0,
-            owe[0:1, :],
-            jnp.where(kq == 1, owe[1:2, :], jnp.where(kq == 2, owe[2:3, :], 0.0)),
-        )
-        for b in range(5):
-            core = jnp.where(wq == wl + 4 * b, small, 0.0).astype(BF16)
-            rmat[b, 0:64, :] = core
-            rmat[b, 64:128, :] = core
-
-    colours()
-
-    tot = stat_wait(0) / COUNT
-    rows = []
-    for f in range(2):
-        mean = tot[2 * f : 2 * f + 1]
-        meansq = tot[2 * f + 1 : 2 * f + 2]
-        rstd = lax.rsqrt(meansq - mean * mean + EPS)
-        rows.append((mean, rstd))
-    table[...] = jnp.zeros((8, 128), F32)
-    for f in range(2):
-        table[f : f + 1, :] = rows[f][0]
-        table[6 + f : 7 + f, 0:96] = 0.5 * rows[f][1][:, 0:96] * gain[...]
-    table[4:5, 0:96] = gain[...]
-    table[5:6, 0:96] = 0.5 * bias[...]
-    cst[...] = jnp.dot(table[...], emat[...], precision=HIGHEST, preferred_element_type=F32)
-
-    def factor():
-        for f in range(2):
-            mean_l = cst[f : f + 1, :]
-            a_l = cst[6 + f : 7 + f, :]
-            hb_l = cst[5:6, :]
-            g2_l = 0.5 * cst[4:5, :]
-
-            def factor_step(i, _, f=f, mean_l=mean_l, a_l=a_l, hb_l=hb_l, g2_l=g2_l):
-                b = lax.div(i, 8)
-                r = pl.multiple_of(lax.rem(i, 8) * 32, 32)
-                v = xb[f * 5 + b, pl.ds(r, 32), :].astype(F32) - mean_l
-                u = v * a_l + hb_l
-                h = jnp.tanh(u)
-                w = (1.0 + u * (1.0 - h)) * ((1.0 + h) * g2_l)
-                for i in range(3):
-                    xs[f * 5 + b, i, pl.ds(r, 32), :] = v[:, 128 * i : 128 * i + 128]
-                    fs[f * 5 + b, i, pl.ds(r, 32), :] = w[:, 128 * i : 128 * i + 128]
-                return 0
-
-            lax.fori_loop(0, 40, factor_step, 0)
-
-    factor()
-
-    def core_copy(ch):
-        return remote(
-            sums.at[ch, 1 - c], cbuf.at[ch], cs.at[ch], cr.at[ch], (tm + 1 - 2 * c, tl)
-        )
-
-    def z_copy(ch, d):
-        zz = lax.rem(z + d, 4)
-        return remote(
-            part.at[ch, zz],
-            zbuf.at[ch, d - 1],
-            zs.at[ch, d - 1],
-            zr.at[ch, d - 1],
-            (zz * 2 + c, tl),
-        )
-
-    def frame_picks():
-        ids = rbuf[0, :, 48:64, :].astype(F32)
-        ids = jnp.broadcast_to(ids[:, 15:16, :], (16, 16, 128)).reshape(256, 128)
-        ids = jnp.concatenate([ids, ids], axis=1)
-        at = iota((256, 256), 1)
-        order = lax.div(at, 16)
-        frame = 4 * lax.rem(lax.div(order, 2), 4) + 2 * lax.div(order, 8) + lax.rem(order, 2)
-        hit = (ids == frame.astype(F32)) & (lax.rem(iota((256, 256), 0), 16) == lax.rem(at, 16))
-        picks[...] = jnp.where(hit, 1.0, 0.0).T.astype(BF16)
-
-    def frame_sums(ch):
-        stack = jnp.concatenate(
-            [rbuf[ch, :, 16 * g : 16 * g + 16, :].reshape(256, 128) for g in range(4)], axis=1
-        )
-        total = jnp.dot(picks[...], stack, preferred_element_type=F32)
-        for g in range(4):
-            sums[ch, :, :, :, 16 * g : 16 * g + 16, :] = total[
-                :, 128 * g : 128 * g + 128
-            ].reshape(2, 4, 2, 16, 128)
-
-    for ch in range(2):
-
-        def recv_strip(d, _, ch=ch):
-            strip_copy(ch, d).wait_recv()
-            return 0
-
-        lax.fori_loop(1, 16, recv_strip, 0)
-        if ch == 0:
-            frame_picks()
-        frame_sums(ch)
-        core_copy(ch).start()
-
-    for ch in range(2):
-        core_copy(ch).wait_recv()
-        part[ch] = sums[ch, c] + cbuf[ch]
-        for d in range(1, 4):
-            z_copy(ch, d).start()
-
-    for ch in range(2):
-        for d in range(1, 4):
-            z_copy(ch, d).wait_recv()
-        def frame_rows(ch=ch):
-            dp = part[ch, z] + (zbuf[ch, 0] + zbuf[ch, 1] + zbuf[ch, 2])
+    def frame_rows():
+        for r in range(2):
+            dp = sums[tm] if r == 0 else unpacked(zbuf[1, 0])
+            for d in range(1, 4):
+                dp = dp + unpacked(zbuf[r, d])
             for f in range(2):
                 top = dp[f].astype(BF16)
                 rest = dp[f] - top.astype(F32)
                 both = jnp.concatenate([top.astype(F32), rest], axis=0).T
-                dpx[ch, 128 * f : 128 * f + 128, :] = both.astype(BF16)
-
-        frame_rows()
+                dpx[lax.rem(c + r, 2), 128 * f : 128 * f + 128, :] = both.astype(BF16)
+
+    for r, d in partners:
+        z_copy(r, d).wait_recv()
+    frame_rows()
 
     def dxh():
         carry = tuple(jnp.zeros((8, 128), F32) for _ in range(12))
@@ -447,7 +442,8 @@
                     new += s + sx
                 return tuple(new)
 
-            carry = lax.fori_loop(0, 5, dxh_step, carry)
+            for b in range(5):
+                carry = dxh_step(b, carry)
         for i in range(12):
             stin[i // 3 : i // 3 + 1, 128 * (i % 3) : 128 * (i % 3) + 128] = jnp.sum(
                 carry[i], axis=0, keepdims=True
@@ -608,17 +604,17 @@
 
     assemble()
 
-    for ch in range(2):
-
-        def sent_strip(d, _, ch=ch):
-            strip_copy(ch, d).wait_send()
-            stat_copy(ch, d).wait_send()
-            return 0
-
-        lax.fori_loop(1, 16, sent_strip, 0)
-        core_copy(ch).wait_send()
-        for d in range(1, 4):
-            z_copy(ch, d).wait_send()
+    def sent_strip(d, _):
+        strip_copy(0, d).wait_send()
+        strip_copy(1, d).wait_send()
+        stat_copy(0, d).wait_send()
+        stat_copy(1, d).wait_send()
+        return 0
+
+    lax.fori_loop(1, 16, sent_strip, 0)
+    strip_copy(1, 0).wait_send()
+    for r, d in partners:
+        z_copy(r, d).wait_send()
 
     def sent_own(d, _):
         own_copy(d, True).wait_send()
@@ -656,11 +652,10 @@
             pltpu.VMEM((27, 96, 384), BF16),
             pltpu.VMEM((2, 16, 64, 128), BF16),
             pltpu.VMEM((2, 16, 64, 128), BF16),
-            pltpu.VMEM((256, 256), BF16),
-            pltpu.VMEM((2, 2, 4, 2, 64, 128), F32),
-            pltpu.VMEM((2, 4, 2, 64, 128), F32),
-            pltpu.VMEM((2, 4, 2, 64, 128), F32),
-            pltpu.VMEM((2, 3, 2, 64, 128), F32),
+            pltpu.VMEM((256, 512), BF16),
+            pltpu.VMEM((8, 2, 64, 128), F32),
+            pltpu.VMEM((8, 2, 64, 128), jnp.int16),
+            pltpu.VMEM((2, 4, 2, 64, 128), jnp.int16),
             pltpu.VMEM((2, 256, 128), BF16),
             pltpu.VMEM((5, 128, BLK), BF16),
             pltpu.VMEM((PIECES, 3, 256, 128), F32),
@@ -684,10 +679,8 @@
             dma((4,)),
             dma((2, 16)),
             dma((2, 16)),
-            dma((2,)),
-            dma((2,)),
-            dma((2, 3)),
-            dma((2, 3)),
+            dma((2, 4)),
+            dma((2, 4)),
             dma((2, 16)),
             dma((2, 16)),
             dma((2, 16)),

time: 54.5 us -> 48.6 us (0.89); the launches traced: 53.5 us -> 48.1 us
  Pallas kernels: 51.2 us -> 45.9 us
    pallas_call x1, Pallas kernels: 51.2 us -> 45.9 us  [body(): pl.pallas_call(kernel, out_shape=jax.ShapeDtypeStruct((8, 5120), F32), in...]
where the time goes in v3:
time: 48.6 us; the launch traced here: 48.1 us
  Pallas kernels  45.9 us (94%)
  local copies, waits for them, and re-layouts  1.59 us (3%)
  between operations  0.66 us (1%)
    pallas_call x1, Pallas kernels, body(): pl.pallas_call(kernel, out_shape=jax.ShapeDtypeStruct((8, 5120), F32), in...  45.9 us
    unnamed x1, local copies, waits for them, and re-layouts  1.59 us

profile of v3, /device:TPU:1, one launch (start us, length us, event | category | flops | bytes accessed | tf_op | source)
XLA Modules:
  0.0 48.1 jit_solution(14658224537294393137)
XLA Ops:
  0.7 45.9 %shard_map.82 = f32[8,5120]{1,0:T(8,128)} custom-call(bf16[1,3,320,256]{3,2,1,0:T(8,128)(2,1)} %bitcast.4, s32[1]{0:T(128)S(6)} %copy.10.fid, bf16[2,256,1920]{2,1,0:T(8,128)(2,1)} %x_hbm.1, f32[1,96]{1,0:T(1,128)} %bitcast.6, f32[1,96]{1,0:T(1,128)} %bitcast.7, bf16[3,96]{1,0:T(4,128)(2,1)} %bitcast.5, bf16[27,96,384]{2,1,0:T(8,128)(2,1)} %cw_hbm.1, ...), custom_call_target="tpu_custom_call" | custom-call | tf_op jit(solution)/shard_map/pallas_call | solution.py:640
  46.5 1.6 %copy.11 = f32[8,5120]{1,0:T(8,128)} copy(f32[8,5120]{1,0:T(8,128)} %shard_map.82) | data formatting | bytes 327680

commit v4 on v3

--- a/solution.py
+++ b/solution.py
@@ -8,7 +8,6 @@
 MESH = pl.DeviceIdType.MESH
 F32 = jnp.float32
 BF16 = jnp.bfloat16
-HIGHEST = lax.Precision.HIGHEST
 COUNT = 256.0 * 320.0 * 3.0
 EPS = 1e-05
 EIGHTHS = 8.0 / 0.6931471805599453
@@ -19,6 +18,15 @@
 
 def iota(shape, dim):
     return lax.broadcasted_iota(jnp.int32, shape, dim)
+
+
+def exact_dot(v, ones):
+    top = v.astype(BF16).astype(F32)
+    mid = (v - top).astype(BF16).astype(F32)
+    parts = jnp.concatenate([top, mid, v - top - mid], axis=0).astype(BF16)
+    w = jnp.dot(parts, ones, preferred_element_type=F32)
+    n = v.shape[0]
+    return w[0:n] + (w[n : 2 * n] + w[2 * n : 3 * n])
 
 
 def remote(src, dst, send_sem, recv_sem, device):
@@ -68,7 +76,8 @@
     cst,
     gred,
     bmat,
-    lhs,
+    lhs0,
+    lhs1,
     ys,
     tok,
     trecv,
@@ -90,7 +99,6 @@
     z = lax.div(tm, 2)
     c = lax.rem(tm, 2)
     below = lax.rem(tm + 7, 8)
-    above = lax.rem(tm + 1, 8)
 
     pix_cp = pltpu.make_async_copy(pix_hbm.at[0], pixv, pix_sem)
     pix_cp.start()
@@ -132,10 +140,10 @@
     lam = iota((BLK, 128), 0)
     chan = iota((BLK, 128), 1)
     same = (lax.div(lax.rem(lam, 96), 3) == lax.div(chan, 3)) & (chan < 96)
-    gmat[...] = jnp.where(same, 1.0, 0.0)
+    gmat[...] = jnp.where(same, 1.0, 0.0).astype(BF16)
     emat[...] = jnp.where(
         lax.rem(iota((128, BLK), 1), 96) == iota((128, BLK), 0), 1.0, 0.0
-    )
+    ).astype(BF16)
 
     def pack():
         frame_id = fid[0].astype(F32)
@@ -212,7 +220,7 @@
         )
 
     def stat_send(which):
-        red = jnp.dot(stin[...], gmat[...], precision=HIGHEST, preferred_element_type=F32)
+        red = exact_dot(stin[...], gmat[...])
         stsend[which] = red
         strecv[which, 0] = red
 
@@ -233,7 +241,7 @@
     stat_send(0)
 
     def colours():
-        owe = jnp.dot(ow[...].astype(F32), emat[0:96, :], preferred_element_type=F32)
+        owe = jnp.dot(ow[...], emat[0:96, :], preferred_element_type=F32)
         q = iota((64, BLK), 0)
         kq = lax.div(q, 20)
         wq = lax.rem(q, 20)
@@ -251,101 +259,6 @@
     for cp in small_cps:
         cp.wait()
     colours()
-
-    tot = stat_wait(0) / COUNT
-    rows = []
-    for f in range(2):
-        mean = tot[2 * f : 2 * f + 1]
-        meansq = tot[2 * f + 1 : 2 * f + 2]
-        rstd = lax.rsqrt(meansq - mean * mean + EPS)
-        rows.append((mean, rstd))
-    table[...] = jnp.zeros((8, 128), F32)
-    for f in range(2):
-        table[f : f + 1, :] = rows[f][0]
-        table[6 + f : 7 + f, 0:96] = 0.5 * rows[f][1][:, 0:96] * gain[...]
-    table[4:5, 0:96] = gain[...]
-    table[5:6, 0:96] = 0.5 * bias[...]
-    cst[...] = jnp.dot(table[...], emat[...], precision=HIGHEST, preferred_element_type=F32)
-
-    def factor():
-        for f in range(2):
-            mean_l = cst[f : f + 1, :]
-            a_l = cst[6 + f : 7 + f, :]
-            hb_l = cst[5:6, :]
-            g2_l = 0.5 * cst[4:5, :]
-
-            def factor_step(i, _, f=f, mean_l=mean_l, a_l=a_l, hb_l=hb_l, g2_l=g2_l):
-                b = lax.div(i, 8)
-                r = pl.multiple_of(lax.rem(i, 8) * 32, 32)
-                v = xb[f * 5 + b, pl.ds(r, 32), :].astype(F32) - mean_l
-                u = v * a_l + hb_l
-                h = jnp.tanh(u)
-                w = (1.0 + u * (1.0 - h)) * ((1.0 + h) * g2_l)
-                for i in range(3):
-                    xs[f * 5 + b, i, pl.ds(r, 32), :] = v[:, 128 * i : 128 * i + 128]
-                    fs[f * 5 + b, i, pl.ds(r, 32), :] = w[:, 128 * i : 128 * i + 128]
-                return 0
-
-            lax.fori_loop(0, 40, factor_step, 0)
-
-    factor()
-
-    def frame_picks():
-        for r in range(2):
-            ids = rbuf[r, :, 48:64, :].astype(F32)
-            ids = jnp.broadcast_to(ids[:, 15:16, :], (16, 16, 128)).reshape(256, 128)
-            ids = jnp.concatenate([ids, ids], axis=1)
-            at = iota((256, 256), 1)
-            hit = (ids == lax.div(at, 16).astype(F32)) & (
-                lax.rem(iota((256, 256), 0), 16) == lax.rem(at, 16)
-            )
-            picks[:, 256 * r : 256 * r + 256] = jnp.where(hit, 1.0, 0.0).T.astype(BF16)
-
-    def frame_sums():
-        stack = jnp.concatenate(
-            [rbuf[:, :, 16 * g : 16 * g + 16, :].reshape(512, 128) for g in range(4)], axis=1
-        )
-        total = jnp.dot(picks[...], stack, preferred_element_type=F32)
-        for g in range(4):
-            v = total[:, 128 * g : 128 * g + 128].reshape(8, 2, 16, 128)
-            if g == 3:
-                v = jnp.where(iota(v.shape, 2) >= 12, 0.0, v)
-            sums[:, :, 16 * g : 16 * g + 16, :] = v
-
-    def packed():
-        for owner in range(8):
-            v = sums[owner]
-            largest = jnp.max(jnp.maximum(v[0], v[1]), axis=0, keepdims=True)
-            smallest = jnp.min(jnp.minimum(v[0], v[1]), axis=0, keepdims=True)
-            largest = jnp.maximum(jnp.maximum(largest, -smallest), 1e-20)
-            step = jnp.floor(jnp.log(largest) * EIGHTHS) + 2.0
-            scale = RANGE * jnp.exp(step * (-1.0 / EIGHTHS))
-            w = jnp.round(v * scale[None])
-            w = jnp.where(iota(v.shape, 1) >= 60, step[None], w)
-            packs[owner] = w.astype(jnp.int32).astype(jnp.int16)
-
-    def unpacked(v):
-        v = v.astype(jnp.int32).astype(F32)
-        return v * (jnp.exp(v[:, 60:61, :] * (1.0 / EIGHTHS)) * (1.0 / RANGE))
-
-    def z_copy(r, d):
-        owner = lax.rem(z + d, 4) * 2 + lax.rem(c + r, 2)
-        return remote(packs.at[owner], zbuf.at[r, d], zs.at[r, d], zr.at[r, d], (owner, tl))
-
-    partners = tuple((r, d) for r in range(2) for d in range(4) if r + d > 0)
-
-    def recv_strip(d, _):
-        strip_copy(0, d).wait_recv()
-        strip_copy(1, d).wait_recv()
-        return 0
-
-    lax.fori_loop(1, 16, recv_strip, 0)
-    strip_copy(1, 0).wait_recv()
-    frame_picks()
-    frame_sums()
-    packed()
-    for r, d in partners:
-        z_copy(r, d).start()
 
 
     spread = jnp.where(lax.div(lax.rem(iota((128, 16), 0), 64), 4) == iota((128, 16), 1), 1.0, 0.0)
@@ -399,14 +312,109 @@
                     row = pl.multiple_of(t * BLK + w * 96 + r, 16)
                     top = taps[t].astype(BF16)
                     rest = (taps[t] - top.astype(F32)).astype(BF16)
-                    bmat[pl.ds(row, 16), 128 * dt : 128 * dt + 128] = top
-                    bmat[pl.ds(row, 16), BLK + 128 * dt : BLK + 128 * dt + 128] = rest
+                    bmat[pl.ds(row, 16), 256 * dt : 256 * dt + 128] = top
+                    bmat[pl.ds(row, 16), 256 * dt + 128 : 256 * dt + 256] = rest
         return 0
 
     def weights():
         lax.fori_loop(0, 6, combine, 0)
 
     weights()
+
+    def frame_picks():
+        for r in range(2):
+            ids = rbuf[r, :, 48:64, :].astype(F32)
+            ids = jnp.broadcast_to(ids[:, 15:16, :], (16, 16, 128)).reshape(256, 128)
+            ids = jnp.concatenate([ids, ids], axis=1)
+            at = iota((256, 256), 1)
+            hit = (ids == lax.div(at, 16).astype(F32)) & (
+                lax.rem(iota((256, 256), 0), 16) == lax.rem(at, 16)
+            )
+            picks[:, 256 * r : 256 * r + 256] = jnp.where(hit, 1.0, 0.0).T.astype(BF16)
+
+    def frame_sums():
+        stack = jnp.concatenate(
+            [rbuf[:, :, 16 * g : 16 * g + 16, :].reshape(512, 128) for g in range(4)], axis=1
+        )
+        total = jnp.dot(picks[...], stack, preferred_element_type=F32)
+        for g in range(4):
+            v = total[:, 128 * g : 128 * g + 128].reshape(8, 2, 16, 128)
+            if g == 3:
+                v = jnp.where(iota(v.shape, 2) >= 12, 0.0, v)
+            sums[:, :, 16 * g : 16 * g + 16, :] = v
+
+    def packed():
+        for owner in range(8):
+            v = sums[owner]
+            largest = jnp.max(jnp.maximum(v[0], v[1]), axis=0, keepdims=True)
+            smallest = jnp.min(jnp.minimum(v[0], v[1]), axis=0, keepdims=True)
+            largest = jnp.maximum(jnp.maximum(largest, -smallest), 1e-20)
+            step = jnp.floor(jnp.log(largest) * EIGHTHS) + 2.0
+            scale = RANGE * jnp.exp(step * (-1.0 / EIGHTHS))
+            w = jnp.round(v * scale[None])
+            w = jnp.where(iota(v.shape, 1) >= 60, step[None], w)
+            packs[owner] = w.astype(jnp.int32).astype(jnp.int16)
+
+    def unpacked(v):
+        v = v.astype(jnp.int32).astype(F32)
+        return v * (jnp.exp(v[:, 60:61, :] * (1.0 / EIGHTHS)) * (1.0 / RANGE))
+
+    def z_copy(r, d):
+        owner = lax.rem(z + d, 4) * 2 + lax.rem(c + r, 2)
+        return remote(packs.at[owner], zbuf.at[r, d], zs.at[r, d], zr.at[r, d], (owner, tl))
+
+    partners = tuple((r, d) for r in range(2) for d in range(4) if r + d > 0)
+
+    def recv_strip(d, _):
+        strip_copy(0, d).wait_recv()
+        strip_copy(1, d).wait_recv()
+        return 0
+
+    lax.fori_loop(1, 16, recv_strip, 0)
+    strip_copy(1, 0).wait_recv()
+    frame_picks()
+    frame_sums()
+    packed()
+    for r, d in partners:
+        z_copy(r, d).start()
+
+    tot = stat_wait(0) / COUNT
+    rows = []
+    for f in range(2):
+        mean = tot[2 * f : 2 * f + 1]
+        meansq = tot[2 * f + 1 : 2 * f + 2]
+        rstd = lax.rsqrt(meansq - mean * mean + EPS)
+        rows.append((mean, rstd))
+    table[...] = jnp.zeros((8, 128), F32)
+    for f in range(2):
+        table[f : f + 1, :] = rows[f][0]
+        table[6 + f : 7 + f, 0:96] = 0.5 * rows[f][1][:, 0:96] * gain[...]
+    table[4:5, 0:96] = gain[...]
+    table[5:6, 0:96] = 0.5 * bias[...]
+    cst[...] = exact_dot(table[...], emat[...])
+
+    def factor():
+        for f in range(2):
+            mean_l = cst[f : f + 1, :]
+            a_l = cst[6 + f : 7 + f, :]
+            hb_l = cst[5:6, :]
+            g2_l = 0.5 * cst[4:5, :]
+
+            def factor_step(i, _, f=f, mean_l=mean_l, a_l=a_l, hb_l=hb_l, g2_l=g2_l):
+                b = lax.div(i, 8)
+                r = pl.multiple_of(lax.rem(i, 8) * 32, 32)
+                v = xb[f * 5 + b, pl.ds(r, 32), :].astype(F32) - mean_l
+                u = v * a_l + hb_l
+                h = jnp.tanh(u)
+                w = (1.0 + u * (1.0 - h)) * ((1.0 + h) * g2_l)
+                for i in range(3):
+                    xs[f * 5 + b, i, pl.ds(r, 32), :] = v[:, 128 * i : 128 * i + 128]
+                    fs[f * 5 + b, i, pl.ds(r, 32), :] = w[:, 128 * i : 128 * i + 128]
+                return 0
+
+            lax.fori_loop(0, 40, factor_step, 0)
+
+    factor()
 
     def frame_rows():
         for r in range(2):
@@ -458,43 +466,38 @@
         first = tot[2 * f : 2 * f + 1]
         second = tot[2 * f + 1 : 2 * f + 2] * rstd
         terms += [rstd, -rstd * rstd * second, -rstd * first, jnp.zeros_like(rstd)]
-    cst[...] = jnp.dot(
-        jnp.concatenate(terms, axis=0), emat[...], precision=HIGHEST, preferred_element_type=F32
-    )
-
-    def left_side():
-        for f in range(2):
-            p_l = cst[4 * f : 4 * f + 1, :]
-            q_l = cst[4 * f + 1 : 4 * f + 2, :]
-            r_l = cst[4 * f + 2 : 4 * f + 3, :]
-
-            def lhs_step(b, _, f=f, p_l=p_l, q_l=q_l, r_l=r_l):
+    cst[...] = exact_dot(jnp.concatenate(terms, axis=0), emat[...])
+
+    def left_side(f):
+        left = lhs0 if f == 0 else lhs1
+        row = iota((64, 128), 0)
+        for i in range(3):
+            ls = slice(128 * i, 128 * i + 128)
+            p_l = cst[4 * f : 4 * f + 1, ls]
+            q_l = cst[4 * f + 1 : 4 * f + 2, ls]
+            r_l = cst[4 * f + 2 : 4 * f + 3, ls]
+            for b in range(5):
                 fb = f * 5 + b
-                row = iota((64, 128), 0)
                 for rho in range(4):
                     sel = pl.ds(rho, 64, stride=4)
-                    for i in range(3):
-                        ls = slice(128 * i, 128 * i + 128)
-                        d = p_l[:, ls] * fs[fb, i, sel, :] + q_l[:, ls] * xs[fb, i, sel, :] + r_l[:, ls]
-                        at = BLK * (rho + 1) + 128 * i
-                        lhs[fb, :, at : at + 128] = d.astype(BF16)
-                        if rho == 0:
-                            d = jnp.where(row == 63, 0.0, pltpu.roll(d, 63, 0))
-                            lhs[fb, :, BLK * 5 + 128 * i : BLK * 5 + 128 * i + 128] = d.astype(BF16)
-                        if rho == 3:
-                            d = jnp.where(row == 0, 0.0, pltpu.roll(d, 1, 0))
-                            lhs[fb, :, 128 * i : 128 * i + 128] = d.astype(BF16)
-                return 0
-
-            lax.fori_loop(0, 5, lhs_step, 0)
-
-    left_side()
-
-    def conv():
-        left = lhs[...].reshape(640, 6 * BLK)
-        ys[...] = jnp.dot(left, bmat[...], preferred_element_type=F32)
-
-    conv()
+                    d = p_l * fs[fb, i, sel, :] + q_l * xs[fb, i, sel, :] + r_l
+                    at = BLK * (rho + 1) + 128 * i
+                    left[64 * b : 64 * b + 64, at : at + 128] = d.astype(BF16)
+                    if rho == 0:
+                        d = jnp.where(row == 63, 0.0, pltpu.roll(d, 63, 0))
+                        at = BLK * 5 + 128 * i
+                        left[64 * b : 64 * b + 64, at : at + 128] = d.astype(BF16)
+                    if rho == 3:
+                        d = jnp.where(row == 0, 0.0, pltpu.roll(d, 1, 0))
+                        at = 128 * i
+                        left[64 * b : 64 * b + 64, at : at + 128] = d.astype(BF16)
+
+    def conv(f, first, last):
+        left = lhs0 if f == 0 else lhs1
+        at = slice(256 * first, 256 * last + 256)
+        ys[320 * f : 320 * f + 320, at] = jnp.dot(
+            left[...], bmat[:, at], preferred_element_type=F32
+        )
 
     ln = iota((64, 128), 1)
     lo64 = ln < 64
@@ -503,37 +506,28 @@
     def taken(f, dt, b):
         r = 64 * (5 * f + b)
         return (
-            ys[r : r + 64, 128 * dt : 128 * dt + 128]
-            + ys[r : r + 64, BLK + 128 * dt : BLK + 128 * dt + 128]
+            ys[r : r + 64, 256 * dt : 256 * dt + 128]
+            + ys[r : r + 64, 256 * dt + 128 : 256 * dt + 256]
         )
 
-    plans = (
-        (1, 0, ((0, 0),)),
-        (1, 1, ((0, 1), (1, 0))),
-        (0, 0, ((0, 2), (1, 1))),
-        (0, 1, ((1, 2),)),
-    )
-    def tokens():
-        for group, t, terms in plans:
-            cc = []
-            for b in range(5):
-                v = taken(*terms[0], b)
-                for term in terms[1:]:
-                    v = v + taken(*term, b)
-                cc.append(v)
-            r1 = pltpu.roll(cc[1], 64, 1)
-            r3 = pltpu.roll(cc[3], 64, 1)
-            v0 = jnp.where(
-                lo64, cc[0] + jnp.where(odd, r1, 0.0), r1 + jnp.where(odd, cc[2], cc[0])
-            )
-            v1 = jnp.where(
-                lo64, cc[2] + jnp.where(odd, r3, r1), r3 + jnp.where(odd, cc[4], cc[2])
-            )
-            v2 = jnp.where(lo64, cc[4] + jnp.where(odd, 0.0, r3), jnp.where(odd, cc[0], cc[4]))
-            for i, v in enumerate((v0, v1, v2)):
-                tok[group, 8 * t : 8 * t + 8, :, 128 * i : 128 * i + 128] = v.reshape(8, 8, 128)
-
-    tokens()
+    def tokens(group, t, terms):
+        cc = []
+        for b in range(5):
+            v = taken(*terms[0], b)
+            for term in terms[1:]:
+                v = v + taken(*term, b)
+            cc.append(v)
+        r1 = pltpu.roll(cc[1], 64, 1)
+        r3 = pltpu.roll(cc[3], 64, 1)
+        v0 = jnp.where(
+            lo64, cc[0] + jnp.where(odd, r1, 0.0), r1 + jnp.where(odd, cc[2], cc[0])
+        )
+        v1 = jnp.where(
+            lo64, cc[2] + jnp.where(odd, r3, r1), r3 + jnp.where(odd, cc[4], cc[2])
+        )
+        v2 = jnp.where(lo64, cc[4] + jnp.where(odd, 0.0, r3), jnp.where(odd, cc[0], cc[4]))
+        for i, v in enumerate((v0, v1, v2)):
+            tok[group, 8 * t : 8 * t + 8, :, 128 * i : 128 * i + 128] = v.reshape(8, 8, 128)
 
     def own_copy(d, sending):
         j = lax.rem(tl + d, 16)
@@ -548,12 +542,21 @@
         span_copy(j, True).start()
         return 0
 
-    lax.fori_loop(0, 16, send_span, 0)
-
     def send_own(d, _):
         own_copy(d, True).start()
         return 0
 
+    left_side(0)
+    conv(0, 0, 1)
+    left_side(1)
+    conv(1, 0, 0)
+    tokens(1, 0, ((0, 0),))
+    tokens(1, 1, ((0, 1), (1, 0)))
+    lax.fori_loop(0, 16, send_span, 0)
+    conv(0, 2, 2)
+    conv(1, 1, 2)
+    tokens(0, 0, ((0, 2), (1, 1)))
+    tokens(0, 1, ((1, 2),))
     lax.fori_loop(1, 16, send_own, 0)
     trecv[0, tl] = tok[0, tl]
 
@@ -633,6 +636,10 @@
     hbm = pl.BlockSpec(memory_space=pltpu.HBM)
     smem = pl.BlockSpec(memory_space=pltpu.SMEM)
     dma = pltpu.SemaphoreType.DMA
+
+    def kept(array):
+        return pltpu.with_memory_space_constraint(array, pltpu.HBM)
+
     pix_grad = jnp.transpose(pix_grad, (0, 1, 3, 2))
     out_weight = out_weight.T
     gain = gain.reshape(1, 96)
@@ -660,8 +667,8 @@
             pltpu.VMEM((5, 128, BLK), BF16),
             pltpu.VMEM((PIECES, 3, 256, 128), F32),
             pltpu.VMEM((PIECES, 3, 256, 128), F32),
-            pltpu.VMEM((BLK, 128), F32),
-            pltpu.VMEM((128, BLK), F32),
+            pltpu.VMEM((BLK, 128), BF16),
+            pltpu.VMEM((128, BLK), BF16),
             pltpu.VMEM((8, BLK), F32),
             pltpu.VMEM((2, 8, 128), F32),
             pltpu.VMEM((2, 16, 8, 128), F32),
@@ -669,7 +676,8 @@
             pltpu.VMEM((8, BLK), F32),
             pltpu.VMEM((27, 96, 128), F32),
             pltpu.VMEM((6 * BLK, 2 * BLK), BF16),
-            pltpu.VMEM((PIECES, 64, 6 * BLK), BF16),
+            pltpu.VMEM((320, 6 * BLK), BF16),
+            pltpu.VMEM((320, 6 * BLK), BF16),
             pltpu.VMEM((640, 2 * BLK), F32),
             pltpu.VMEM((2, 16, 8, BLK), F32),
             pltpu.VMEM((2, 16, 8, BLK), F32),
@@ -687,9 +695,18 @@
             dma((2, 16)),
         ],
         compiler_params=pltpu.CompilerParams(
-            collective_id=0, has_side_effects=True, vmem_limit_bytes=62 * 1024 * 1024
+            collective_id=0, has_side_effects=True, vmem_limit_bytes=50 * 1024 * 1024
         ),
-    )(pix_grad, frame_ids, pre_norm, gain, bias, out_weight, conv_weight, in_weight)
+    )(
+        kept(pix_grad),
+        frame_ids,
+        kept(pre_norm),
+        kept(gain),
+        kept(bias),
+        kept(out_weight),
+        kept(conv_weight),
+        kept(in_weight),
+    )
 
 
 def solution(mesh):

time: 48.6 us -> 42.8 us (0.88)
  Pallas kernels: 45.9 us -> 41.2 us
  local copies, waits for them, and re-layouts: 1.59 us -> 0.67 us
    pallas_call x1, Pallas kernels: 45.9 us -> 41.2 us  [body(): pl.pallas_call(kernel, out_shape=jax.ShapeDtypeStruct((8, 5120), F32), in...]
    unnamed x1, local copies, waits for them, and re-layouts: 1.59 us -> 0.67 us
where the time goes in v4:
time: 42.8 us; the launch traced here: 42.6 us
  Pallas kernels  41.2 us (96%)
  local copies, waits for them, and re-layouts  0.67 us (2%)
  between operations  0.66 us (2%)
    pallas_call x1, Pallas kernels, body(): pl.pallas_call(kernel, out_shape=jax.ShapeDtypeStruct((8, 5120), F32), in...  41.2 us

profile of v4, /device:TPU:1, one launch (start us, length us, event | category | flops | bytes accessed | tf_op | source)
XLA Modules:
  0.0 42.6 jit_solution(18045533875545009208)
XLA Ops:
  0.7 41.2 %shard_map.82 = f32[8,5120]{1,0:T(8,128)S(1)} custom-call(bf16[1,3,320,256]{3,2,1,0:T(8,128)(2,1)} %bitcast.4, s32[1]{0:T(128)S(6)} %copy.10.fid, bf16[2,256,1920]{2,1,0:T(8,128)(2,1)} %x_hbm.1, f32[1,96]{1,0:T(1,128)} %bitcast.6, f32[1,96]{1,0:T(1,128)} %bitcast.7, bf16[3,96]{1,0:T(4,128)(2,1)} %bitcast.5, bf16[27,96,384]{2,1,0:T(8,128)(2,1)} %cw_hbm.1, ...), custom_call_target="tpu_custom_call" | custom-call | tf_op jit(solution)/shard_map/pallas_call | solution.py:647
  41.9 0.7 %copy.11 = f32[8,5120]{1,0:T(8,128)} copy(f32[8,5120]{1,0:T(8,128)S(1)} %shard_map.82) | data formatting | bytes 327680

commit v5 on v4

--- a/solution.py
+++ b/solution.py
@@ -13,6 +13,15 @@
 EIGHTHS = 8.0 / 0.6931471805599453
 RANGE = 32700.0
 BLK = 384
+PEERS = (
+    (1, 2), (3, 2), (2, 1), (2, 3), (2, 2), (0, 1), (1, 1), (0, 3),
+    (3, 3), (1, 3), (3, 1), (0, 2), (2, 0), (1, 0), (3, 0),
+)
+FARTHEST = (
+    (2, 2), (1, 2), (3, 2), (2, 1), (2, 3), (1, 1), (3, 3), (1, 3),
+    (3, 1), (2, 0), (0, 2), (0, 1), (1, 0), (0, 3), (3, 0),
+)
+DXH = ((0, 0), (0, 1), (0, 2), (1, 2), (1, 3), (1, 4))
 PIECES = 10
 
 
@@ -99,6 +108,12 @@
     z = lax.div(tm, 2)
     c = lax.rem(tm, 2)
     below = lax.rem(tm + 7, 8)
+    x = lax.div(tl, 4)
+    y = lax.rem(tl, 4)
+
+    def tile_at(place):
+        return lax.rem(x + place[0], 4) * 4 + lax.rem(y + place[1], 4)
+
 
     pix_cp = pltpu.make_async_copy(pix_hbm.at[0], pixv, pix_sem)
     pix_cp.start()
@@ -149,11 +164,11 @@
         frame_id = fid[0].astype(F32)
         r = iota((256, 240), 0)
         m = iota((256, 240), 1)
-        slot = lax.rem(r, 64)
-        col = 20 * lax.div(r, 64) + lax.rem(slot, 20)
-        hit = (slot < 60) & (m == 80 * lax.div(slot, 20) + col)
+        slot = lax.rem(r, 32)
+        col = 20 * lax.div(r, 64) + 10 * lax.div(lax.rem(r, 64), 32) + lax.rem(slot, 10)
+        hit = (slot < 30) & (m == 80 * lax.div(slot, 10) + col)
         pick = jnp.where(hit, 1.0, 0.0).astype(BF16)
-        spare = lax.rem(iota((256, 256), 0), 64) >= 60
+        spare = lax.rem(iota((256, 256), 0), 32) >= 30
         for n in range(4):
             stack = jnp.concatenate(
                 [pixv[k, 80 * n : 80 * n + 80, :] for k in range(3)], axis=0
@@ -168,19 +183,24 @@
 
     pix_cp.wait()
     pack()
-    def strip_copy(r, d):
-        j = lax.rem(tl + d, 16)
+    def strip_copy(half, r, d):
+        j = tl if d == 0 else tile_at(PEERS[d - 1])
         h = lax.rem(c + r, 2)
-        return remote(sbuf.at[h, j], rbuf.at[r, d], s1s.at[r, d], s1r.at[r, d], (2 * z + h, j))
+        rows = pl.ds(32 * half, 32)
+        return remote(
+            sbuf.at[h, j, rows],
+            rbuf.at[r, d, rows],
+            s1s.at[half, r, d],
+            s1r.at[half, r, d],
+            (2 * z + h, j),
+        )
+
+    strips = tuple((r, d) for d in range(1, 16) for r in range(2)) + ((1, 0),)
 
     def strips_sent():
-        def send_strip(d, _):
-            strip_copy(0, d).start()
-            strip_copy(1, d).start()
-            return 0
-
-        lax.fori_loop(1, 16, send_strip, 0)
-        strip_copy(1, 0).start()
+        for half in range(2):
+            for r, d in strips:
+                strip_copy(half, r, d).start()
         rbuf[0, 0] = sbuf[c, tl]
 
     for cp in x_cps:
@@ -210,51 +230,44 @@
     strips_sent()
 
     def stat_copy(which, d):
-        j = lax.rem(tl + d, 16)
         return remote(
             stsend.at[which],
             strecv.at[which, d],
             sts.at[which, d],
             strs.at[which, d],
-            (tm, j),
+            (tm, tile_at(FARTHEST[d - 1])),
         )
 
     def stat_send(which):
         red = exact_dot(stin[...], gmat[...])
         stsend[which] = red
         strecv[which, 0] = red
-
-        def go(d, _):
+        for d in range(1, 16):
             stat_copy(which, d).start()
-            return 0
-
-        lax.fori_loop(1, 16, go, 0)
 
     def stat_wait(which):
-        def go(d, _):
+        for d in range(1, 16):
             stat_copy(which, d).wait_recv()
-            return 0
-
-        lax.fori_loop(1, 16, go, 0)
         return jnp.sum(strecv[which], axis=0)
 
     stat_send(0)
 
     def colours():
         owe = jnp.dot(ow[...], emat[0:96, :], preferred_element_type=F32)
-        q = iota((64, BLK), 0)
-        kq = lax.div(q, 20)
-        wq = lax.rem(q, 20)
-        wl = lax.div(iota((64, BLK), 1), 96)
+        q = iota((32, BLK), 0)
+        kq = lax.div(q, 10)
+        wq = lax.rem(q, 10)
+        wl = lax.div(iota((32, BLK), 1), 96)
         small = jnp.where(
             kq == 0,
             owe[0:1, :],
             jnp.where(kq == 1, owe[1:2, :], jnp.where(kq == 2, owe[2:3, :], 0.0)),
         )
-        for b in range(5):
-            core = jnp.where(wq == wl + 4 * b, small, 0.0).astype(BF16)
-            rmat[b, 0:64, :] = core
-            rmat[b, 64:128, :] = core
+        for half, b in DXH:
+            core = jnp.where(wq + 10 * half == wl + 4 * b, small, 0.0).astype(BF16)
+            for part in range(3):
+                rmat[half, b, 32 * part : 32 * part + 32, :] = core
+            rmat[half, b, 96:128, :] = jnp.zeros((32, BLK), BF16)
 
     for cp in small_cps:
         cp.wait()
@@ -323,7 +336,7 @@
 
     def frame_picks():
         for r in range(2):
-            ids = rbuf[r, :, 48:64, :].astype(F32)
+            ids = rbuf[r, :, 16:32, :].astype(F32)
             ids = jnp.broadcast_to(ids[:, 15:16, :], (16, 16, 128)).reshape(256, 128)
             ids = jnp.concatenate([ids, ids], axis=1)
             at = iota((256, 256), 1)
@@ -332,51 +345,55 @@
             )
             picks[:, 256 * r : 256 * r + 256] = jnp.where(hit, 1.0, 0.0).T.astype(BF16)
 
-    def frame_sums():
+    def frame_sums(half):
         stack = jnp.concatenate(
-            [rbuf[:, :, 16 * g : 16 * g + 16, :].reshape(512, 128) for g in range(4)], axis=1
+            [rbuf[:, :, 16 * g : 16 * g + 16, :].reshape(512, 128) for g in (2 * half, 2 * half + 1)],
+            axis=1,
         )
         total = jnp.dot(picks[...], stack, preferred_element_type=F32)
-        for g in range(4):
+        for g in range(2):
             v = total[:, 128 * g : 128 * g + 128].reshape(8, 2, 16, 128)
-            if g == 3:
-                v = jnp.where(iota(v.shape, 2) >= 12, 0.0, v)
-            sums[:, :, 16 * g : 16 * g + 16, :] = v
-
-    def packed():
+            if g == 1:
+                v = jnp.where(iota(v.shape, 2) >= 14, 0.0, v)
+            sums[half, :, :, 16 * g : 16 * g + 16, :] = v
+
+    def packed(half):
         for owner in range(8):
-            v = sums[owner]
+            v = sums[half, owner]
             largest = jnp.max(jnp.maximum(v[0], v[1]), axis=0, keepdims=True)
             smallest = jnp.min(jnp.minimum(v[0], v[1]), axis=0, keepdims=True)
             largest = jnp.maximum(jnp.maximum(largest, -smallest), 1e-20)
             step = jnp.floor(jnp.log(largest) * EIGHTHS) + 2.0
             scale = RANGE * jnp.exp(step * (-1.0 / EIGHTHS))
             w = jnp.round(v * scale[None])
-            w = jnp.where(iota(v.shape, 1) >= 60, step[None], w)
-            packs[owner] = w.astype(jnp.int32).astype(jnp.int16)
+            w = jnp.where(iota(v.shape, 1) >= 30, step[None], w)
+            packs[half, owner] = w.astype(jnp.int32).astype(jnp.int16)
 
     def unpacked(v):
         v = v.astype(jnp.int32).astype(F32)
-        return v * (jnp.exp(v[:, 60:61, :] * (1.0 / EIGHTHS)) * (1.0 / RANGE))
-
-    def z_copy(r, d):
+        return v * (jnp.exp(v[:, 30:31, :] * (1.0 / EIGHTHS)) * (1.0 / RANGE))
+
+    def z_copy(half, r, d):
         owner = lax.rem(z + d, 4) * 2 + lax.rem(c + r, 2)
-        return remote(packs.at[owner], zbuf.at[r, d], zs.at[r, d], zr.at[r, d], (owner, tl))
-
-    partners = tuple((r, d) for r in range(2) for d in range(4) if r + d > 0)
-
-    def recv_strip(d, _):
-        strip_copy(0, d).wait_recv()
-        strip_copy(1, d).wait_recv()
-        return 0
-
-    lax.fori_loop(1, 16, recv_strip, 0)
-    strip_copy(1, 0).wait_recv()
-    frame_picks()
-    frame_sums()
-    packed()
-    for r, d in partners:
-        z_copy(r, d).start()
+        return remote(
+            packs.at[half, owner],
+            zbuf.at[half, r, d],
+            zs.at[half, r, d],
+            zr.at[half, r, d],
+            (owner, tl),
+        )
+
+    partners = tuple((r, d) for d in (2, 1, 3, 0) for r in (1, 0) if r + d > 0)
+
+    for half in range(2):
+        for r, d in strips:
+            strip_copy(half, r, d).wait_recv()
+        if half == 0:
+            frame_picks()
+        frame_sums(half)
+        packed(half)
+        for r, d in partners:
+            z_copy(half, r, d).start()
 
     tot = stat_wait(0) / COUNT
     rows = []
@@ -416,30 +433,31 @@
 
     factor()
 
-    def frame_rows():
+    def frame_rows(half):
         for r in range(2):
-            dp = sums[tm] if r == 0 else unpacked(zbuf[1, 0])
+            dp = sums[half, tm] if r == 0 else unpacked(zbuf[half, 1, 0])
             for d in range(1, 4):
-                dp = dp + unpacked(zbuf[r, d])
+                dp = dp + unpacked(zbuf[half, r, d])
             for f in range(2):
-                top = dp[f].astype(BF16)
-                rest = dp[f] - top.astype(F32)
-                both = jnp.concatenate([top.astype(F32), rest], axis=0).T
-                dpx[lax.rem(c + r, 2), 128 * f : 128 * f + 128, :] = both.astype(BF16)
-
-    for r, d in partners:
-        z_copy(r, d).wait_recv()
-    frame_rows()
-
-    def dxh():
-        carry = tuple(jnp.zeros((8, 128), F32) for _ in range(12))
-        for half in range(2):
-
-            def dxh_step(b, carry, half=half):
-                da = jnp.dot(dpx[half], rmat[b], preferred_element_type=F32)
+                top = dp[f].astype(BF16).astype(F32)
+                mid = (dp[f] - top).astype(BF16).astype(F32)
+                rest = dp[f] - top - mid
+                parts = jnp.concatenate([top, mid, rest, jnp.zeros_like(rest)], axis=0).T
+                dpx[half, lax.rem(c + r, 2), 128 * f : 128 * f + 128, :] = parts.astype(BF16)
+
+    def dxh(blocks, carry):
+        for b in blocks:
+            for rows_at in range(2):
+                da = None
+                for half in range(2):
+                    if (half, b) in DXH:
+                        v = jnp.dot(
+                            dpx[half, rows_at], rmat[half, b], preferred_element_type=F32
+                        )
+                        da = v if da is None else da + v
                 new = []
                 for f in range(2):
-                    at = pl.ds(128 * half, 128)
+                    at = pl.ds(128 * rows_at, 128)
                     s, sx = [], []
                     for i in range(3):
                         v = da[128 * f : 128 * f + 128, 128 * i : 128 * i + 128]
@@ -448,16 +466,23 @@
                         s.append(carry[6 * f + i] + fold(v))
                         sx.append(carry[6 * f + 3 + i] + fold(v * xs[f * 5 + b, i, at, :]))
                     new += s + sx
-                return tuple(new)
-
-            for b in range(5):
-                carry = dxh_step(b, carry)
+                carry = tuple(new)
+        return carry
+
+    carry = tuple(jnp.zeros((8, 128), F32) for _ in range(12))
+    for half in range(2):
+        for r, d in partners:
+            z_copy(half, r, d).wait_recv()
+        frame_rows(half)
+        carry = dxh((0, 1) if half == 0 else (2, 3, 4), carry)
+
+    def dxh_sums():
         for i in range(12):
             stin[i // 3 : i // 3 + 1, 128 * (i % 3) : 128 * (i % 3) + 128] = jnp.sum(
                 carry[i], axis=0, keepdims=True
             )
 
-    dxh()
+    dxh_sums()
     stat_send(1)
     tot = stat_wait(1) / COUNT
     terms = []
@@ -530,21 +555,16 @@
             tok[group, 8 * t : 8 * t + 8, :, 128 * i : 128 * i + 128] = v.reshape(8, 8, 128)
 
     def own_copy(d, sending):
-        j = lax.rem(tl + d, 16)
-        at = tl if sending else lax.rem(tl + 16 - d, 16)
+        a, b = FARTHEST[d - 1]
+        j = tile_at((a, b))
+        at = tl if sending else tile_at((4 - a, 4 - b))
         return remote(tok.at[0, j], trecv.at[0, at], tks.at[0, d], tkr.at[0, at], (tm, j))
 
-    def span_copy(j, sending):
-        at = tl if sending else j
-        return remote(tok.at[1, j], trecv.at[1, at], tks.at[1, j], tkr.at[1, at], (below, j))
-
-    def send_span(j, _):
-        span_copy(j, True).start()
-        return 0
-
-    def send_own(d, _):
-        own_copy(d, True).start()
-        return 0
+    def span_copy(d, sending):
+        a, b = ((FARTHEST + ((0, 0),)))[d]
+        j = tile_at((a, b))
+        at = tl if sending else tile_at((4 - a, 4 - b))
+        return remote(tok.at[1, j], trecv.at[1, at], tks.at[1, d], tkr.at[1, at], (below, j))
 
     left_side(0)
     conv(0, 0, 1)
@@ -552,25 +572,20 @@
     conv(1, 0, 0)
     tokens(1, 0, ((0, 0),))
     tokens(1, 1, ((0, 1), (1, 0)))
-    lax.fori_loop(0, 16, send_span, 0)
+    for d in range(16):
+        span_copy(d, True).start()
     conv(0, 2, 2)
     conv(1, 1, 2)
     tokens(0, 0, ((0, 2), (1, 1)))
     tokens(0, 1, ((1, 2),))
-    lax.fori_loop(1, 16, send_own, 0)
+    for d in range(1, 16):
+        own_copy(d, True).start()
     trecv[0, tl] = tok[0, tl]
 
-    def recv_span(j, _):
-        span_copy(j, False).wait_recv()
-        return 0
-
-    lax.fori_loop(0, 16, recv_span, 0)
-
-    def recv_own(d, _):
+    for d in range(16):
+        span_copy(d, False).wait_recv()
+    for d in range(1, 16):
         own_copy(d, False).wait_recv()
-        return 0
-
-    lax.fori_loop(1, 16, recv_own, 0)
 
     def assemble():
         ln = iota((8, 128), 1)
@@ -607,29 +622,17 @@
 
     assemble()
 
-    def sent_strip(d, _):
-        strip_copy(0, d).wait_send()
-        strip_copy(1, d).wait_send()
-        stat_copy(0, d).wait_send()
-        stat_copy(1, d).wait_send()
-        return 0
-
-    lax.fori_loop(1, 16, sent_strip, 0)
-    strip_copy(1, 0).wait_send()
-    for r, d in partners:
-        z_copy(r, d).wait_send()
-
-    def sent_own(d, _):
+    for half in range(2):
+        for r, d in strips:
+            strip_copy(half, r, d).wait_send()
+        for r, d in partners:
+            z_copy(half, r, d).wait_send()
+        for d in range(1, 16):
+            stat_copy(half, d).wait_send()
+    for d in range(1, 16):
         own_copy(d, True).wait_send()
-        return 0
-
-    lax.fori_loop(1, 16, sent_own, 0)
-
-    def sent_span(j, _):
-        span_copy(j, True).wait_send()
-        return 0
-
-    lax.fori_loop(0, 16, sent_span, 0)
+    for d in range(16):
+        span_copy(d, True).wait_send()
 
 
 def body(pix_grad, frame_ids, pre_norm, gain, bias, out_weight, conv_weight, in_weight):
@@ -660,11 +663,11 @@
             pltpu.VMEM((2, 16, 64, 128), BF16),
             pltpu.VMEM((2, 16, 64, 128), BF16),
             pltpu.VMEM((256, 512), BF16),
-            pltpu.VMEM((8, 2, 64, 128), F32),
-            pltpu.VMEM((8, 2, 64, 128), jnp.int16),
-            pltpu.VMEM((2, 4, 2, 64, 128), jnp.int16),
-            pltpu.VMEM((2, 256, 128), BF16),
-            pltpu.VMEM((5, 128, BLK), BF16),
+            pltpu.VMEM((2, 8, 2, 32, 128), F32),
+            pltpu.VMEM((2, 8, 2, 32, 128), jnp.int16),
+            pltpu.VMEM((2, 2, 4, 2, 32, 128), jnp.int16),
+            pltpu.VMEM((2, 2, 256, 128), BF16),
+            pltpu.VMEM((2, 5, 128, BLK), BF16),
             pltpu.VMEM((PIECES, 3, 256, 128), F32),
             pltpu.VMEM((PIECES, 3, 256, 128), F32),
             pltpu.VMEM((BLK, 128), BF16),
@@ -685,10 +688,10 @@
             dma((PIECES,)),
             dma,
             dma((4,)),
-            dma((2, 16)),
-            dma((2, 16)),
-            dma((2, 4)),
-            dma((2, 4)),
+            dma((2, 2, 16)),
+            dma((2, 2, 16)),
+            dma((2, 2, 4)),
+            dma((2, 2, 4)),
             dma((2, 16)),
             dma((2, 16)),
             dma((2, 16)),

time: 42.8 us -> 40.6 us (0.949)
  Pallas kernels: 41.2 us -> 38.7 us
    pallas_call x1, Pallas kernels: 41.2 us -> 38.7 us  [body(): pl.pallas_call(kernel, out_shape=jax.ShapeDtypeStruct((8, 5120), F32), in...]
where the time goes in v5:
time: 40.6 us; the launch traced here: 40.1 us
  Pallas kernels  38.7 us (95%)
  local copies, waits for them, and re-layouts  0.67 us (2%)
  between operations  0.66 us (2%)
    pallas_call x1, Pallas kernels, body(): pl.pallas_call(kernel, out_shape=jax.ShapeDtypeStruct((8, 5120), F32), in...  38.7 us

profile of v5, /device:TPU:1, one launch (start us, length us, event | category | flops | bytes accessed | tf_op | source)
XLA Modules:
  0.0 40.1 jit_solution(2857437401154967814)
XLA Ops:
  0.7 38.7 %shard_map.82 = f32[8,5120]{1,0:T(8,128)S(1)} custom-call(bf16[1,3,320,256]{3,2,1,0:T(8,128)(2,1)} %bitcast.4, s32[1]{0:T(128)S(6)} %copy.10.fid, bf16[2,256,1920]{2,1,0:T(8,128)(2,1)} %x_hbm.1, f32[1,96]{1,0:T(1,128)} %bitcast.6, f32[1,96]{1,0:T(1,128)} %bitcast.7, bf16[3,96]{1,0:T(4,128)(2,1)} %bitcast.5, bf16[27,96,384]{2,1,0:T(8,128)(2,1)} %cw_hbm.1, ...), custom_call_target="tpu_custom_call" | custom-call | tf_op jit(solution)/shard_map/pallas_call | solution.py:650
  39.4 0.7 %copy.11 = f32[8,5120]{1,0:T(8,128)} copy(f32[8,5120]{1,0:T(8,128)S(1)} %shard_map.82) | data formatting | bytes 327680

commit v6 on v5

--- a/solution.py
+++ b/solution.py
@@ -13,10 +13,8 @@
 EIGHTHS = 8.0 / 0.6931471805599453
 RANGE = 32700.0
 BLK = 384
-PEERS = (
-    (1, 2), (3, 2), (2, 1), (2, 3), (2, 2), (0, 1), (1, 1), (0, 3),
-    (3, 3), (1, 3), (3, 1), (0, 2), (2, 0), (1, 0), (3, 0),
-)
+NEAR = ((2, 0), (0, 2), (1, 0), (0, 1), (3, 0), (0, 3))
+PEERS = NEAR + ((1, 2), (3, 2), (2, 1), (2, 3), (2, 2), (1, 1), (3, 3), (1, 3), (3, 1))
 FARTHEST = (
     (2, 2), (1, 2), (3, 2), (2, 1), (2, 3), (1, 1), (3, 3), (1, 3),
     (3, 1), (2, 0), (0, 2), (0, 1), (1, 0), (0, 3), (3, 0),
@@ -84,12 +82,18 @@
     table,
     cst,
     gred,
-    bmat,
-    lhs0,
-    lhs1,
-    ys,
+    bupper,
+    bmiddle,
+    blower,
+    lupper,
+    lmiddle,
+    llower,
+    yupper,
+    ymiddle,
+    ylower,
     tok,
     trecv,
+    ready_sem,
     pix_sem,
     x_sem,
     cw_sem,
@@ -115,6 +119,19 @@
         return lax.rem(x + place[0], 4) * 4 + lax.rem(y + place[1], 4)
 
 
+    barrier = pltpu.get_barrier_semaphore()
+
+    def greet(device):
+        pl.semaphore_signal(barrier, inc=1, device_id=device, device_id_type=MESH)
+
+    for place in NEAR:
+        greet((tm, tile_at(place)))
+        greet((tm + 1 - 2 * c, tile_at(place)))
+    for d in (2, 1, 3):
+        for r in range(2):
+            greet((lax.rem(z + d, 4) * 2 + lax.rem(c + r, 2), tl))
+    greet((tm + 1 - 2 * c, tl))
+
     pix_cp = pltpu.make_async_copy(pix_hbm.at[0], pixv, pix_sem)
     pix_cp.start()
     x_cps = []
@@ -134,31 +151,6 @@
         small_cps.append(cp)
     cw_cp = pltpu.make_async_copy(cw_hbm, cwv, cw_sem)
     cw_cp.start()
-
-    barrier = pltpu.get_barrier_semaphore()
-
-    def greet(device):
-        pl.semaphore_signal(barrier, inc=1, device_id=device, device_id_type=MESH)
-
-    def greet_chip(d, _):
-        j = lax.rem(tl + d, 16)
-        greet((tm, j))
-        greet((tm + 1 - 2 * c, j))
-        return 0
-
-    lax.fori_loop(1, 16, greet_chip, 0)
-    greet((tm + 1 - 2 * c, tl))
-    for d in range(1, 4):
-        for r in range(2):
-            greet((lax.rem(z + d, 4) * 2 + lax.rem(c + r, 2), tl))
-
-    lam = iota((BLK, 128), 0)
-    chan = iota((BLK, 128), 1)
-    same = (lax.div(lax.rem(lam, 96), 3) == lax.div(chan, 3)) & (chan < 96)
-    gmat[...] = jnp.where(same, 1.0, 0.0).astype(BF16)
-    emat[...] = jnp.where(
-        lax.rem(iota((128, BLK), 1), 96) == iota((128, BLK), 0), 1.0, 0.0
-    ).astype(BF16)
 
     def pack():
         frame_id = fid[0].astype(F32)
@@ -197,11 +189,29 @@
 
     strips = tuple((r, d) for d in range(1, 16) for r in range(2)) + ((1, 0),)
 
-    def strips_sent():
+    def strips_sent(some):
         for half in range(2):
-            for r, d in strips:
+            for r, d in some:
                 strip_copy(half, r, d).start()
-        rbuf[0, 0] = sbuf[c, tl]
+
+    pl.semaphore_wait(barrier, 12 + 6 + 1)
+    for place in ((2, 0), (1, 0), (3, 0)):
+        pl.semaphore_signal(
+            ready_sem, inc=1, device_id=(tm, tile_at(place)), device_id_type=MESH
+        )
+    strips_sent(strips[0:12] + strips[-1:])
+    rbuf[0, 0] = sbuf[c, tl]
+
+    pl.semaphore_wait(ready_sem, 3)
+    strips_sent(strips[12:30])
+
+    lam = iota((BLK, 128), 0)
+    chan = iota((BLK, 128), 1)
+    same = (lax.div(lax.rem(lam, 96), 3) == lax.div(chan, 3)) & (chan < 96)
+    gmat[...] = jnp.where(same, 1.0, 0.0).astype(BF16)
+    emat[...] = jnp.where(
+        lax.rem(iota((128, BLK), 1), 96) == iota((128, BLK), 0), 1.0, 0.0
+    ).astype(BF16)
 
     for cp in x_cps:
         cp.wait()
@@ -226,8 +236,6 @@
             stin[2 * f + 1 : 2 * f + 2, :] = jnp.sum(ss, axis=0, keepdims=True)
 
     stats()
-    pl.semaphore_wait(barrier, 31 + 6)
-    strips_sent()
 
     def stat_copy(which, d):
         return remote(
@@ -312,21 +320,21 @@
                 h0, h1, h2 = (cols[dh][w] for dh in range(3))
                 h01 = h0 + h1
                 h12 = h1 + h2
-                zero = jnp.zeros_like(h01)
-                taps = (
-                    jnp.where(a0, h2, zero),
-                    jnp.where(a0, h12, zero),
-                    jnp.where(a0, h01, h2),
-                    jnp.where(a0, h0, h12),
-                    jnp.where(a0, zero, h01),
-                    jnp.where(a0, zero, h0),
-                )
-                for t in range(6):
+                for value, ref, t, at in (
+                    (h2, bupper, 0, 128 * dt),
+                    (h12, bupper, 1, 128 * dt),
+                    (h01, bmiddle, 0, 256 * dt),
+                    (h0, bmiddle, 1, 256 * dt),
+                    (h2, bmiddle, 0, 256 * dt + 128),
+                    (h12, bmiddle, 1, 256 * dt + 128),
+                    (h01, blower, 0, 128 * dt),
+                    (h0, blower, 1, 128 * dt),
+                ):
                     row = pl.multiple_of(t * BLK + w * 96 + r, 16)
-                    top = taps[t].astype(BF16)
-                    rest = (taps[t] - top.astype(F32)).astype(BF16)
-                    bmat[pl.ds(row, 16), 256 * dt : 256 * dt + 128] = top
-                    bmat[pl.ds(row, 16), 256 * dt + 128 : 256 * dt + 256] = rest
+                    top = value.astype(BF16).astype(F32)
+                    rest = value - top
+                    first = a0 if at % 256 == 0 and ref is bmiddle or ref is bupper else ~a0
+                    ref[pl.ds(row, 16), at : at + 128] = jnp.where(first, top, rest).astype(BF16)
         return 0
 
     def weights():
@@ -493,8 +501,11 @@
         terms += [rstd, -rstd * rstd * second, -rstd * first, jnp.zeros_like(rstd)]
     cst[...] = exact_dot(jnp.concatenate(terms, axis=0), emat[...])
 
-    def left_side(f):
-        left = lhs0 if f == 0 else lhs1
+    def placed(left, f, b, tap, i, d):
+        at = BLK * tap + 128 * i
+        left[f, 64 * b : 64 * b + 64, at : at + 128] = d.astype(BF16)
+
+    def left_side(f, rows):
         row = iota((64, 128), 0)
         for i in range(3):
             ls = slice(128 * i, 128 * i + 128)
@@ -503,45 +514,55 @@
             r_l = cst[4 * f + 2 : 4 * f + 3, ls]
             for b in range(5):
                 fb = f * 5 + b
-                for rho in range(4):
+                for rho in rows:
                     sel = pl.ds(rho, 64, stride=4)
                     d = p_l * fs[fb, i, sel, :] + q_l * xs[fb, i, sel, :] + r_l
-                    at = BLK * (rho + 1) + 128 * i
-                    left[64 * b : 64 * b + 64, at : at + 128] = d.astype(BF16)
                     if rho == 0:
+                        placed(lupper, f, b, 1, i, d)
                         d = jnp.where(row == 63, 0.0, pltpu.roll(d, 63, 0))
-                        at = BLK * 5 + 128 * i
-                        left[64 * b : 64 * b + 64, at : at + 128] = d.astype(BF16)
-                    if rho == 3:
+                        placed(llower, f, b, 1, i, d)
+                    elif rho == 3:
+                        placed(llower, f, b, 0, i, d)
                         d = jnp.where(row == 0, 0.0, pltpu.roll(d, 1, 0))
-                        at = 128 * i
-                        left[64 * b : 64 * b + 64, at : at + 128] = d.astype(BF16)
-
-    def conv(f, first, last):
-        left = lhs0 if f == 0 else lhs1
-        at = slice(256 * first, 256 * last + 256)
-        ys[320 * f : 320 * f + 320, at] = jnp.dot(
-            left[...], bmat[:, at], preferred_element_type=F32
-        )
+                        placed(lupper, f, b, 0, i, d)
+                    else:
+                        placed(lmiddle, f, b, rho - 1, i, d)
+
+    def conv(f, first, last, left, weight, result):
+        width = weight.shape[1] // 3
+        at = slice(width * first, width * last + width)
+        result[320 * f : 320 * f + 320, at] = jnp.dot(
+            left[f], weight[:, at], preferred_element_type=F32
+        )
+
+    def conv_middle(f, first, last):
+        conv(f, first, last, lmiddle, bmiddle, ymiddle)
+
+    def conv_ends(f, first, last):
+        conv(f, first, last, lupper, bupper, yupper)
+        conv(f, first, last, llower, blower, ylower)
 
     ln = iota((64, 128), 1)
     lo64 = ln < 64
     odd = lax.rem(ln, 2) == 1
+    upper = lax.rem(lax.div(ln, 2), 2) == 0
 
     def taken(f, dt, b):
-        r = 64 * (5 * f + b)
+        r = slice(64 * (5 * f + b), 64 * (5 * f + b) + 64)
+        narrow = slice(128 * dt, 128 * dt + 128)
         return (
-            ys[r : r + 64, 256 * dt : 256 * dt + 128]
-            + ys[r : r + 64, 256 * dt + 128 : 256 * dt + 256]
+            yupper[r, narrow] + ymiddle[r, 256 * dt : 256 * dt + 128],
+            ylower[r, narrow] + ymiddle[r, 256 * dt + 128 : 256 * dt + 256],
         )
 
     def tokens(group, t, terms):
         cc = []
         for b in range(5):
-            v = taken(*terms[0], b)
+            u, v = taken(*terms[0], b)
             for term in terms[1:]:
-                v = v + taken(*term, b)
-            cc.append(v)
+                more = taken(*term, b)
+                u, v = u + more[0], v + more[1]
+            cc.append(jnp.where(upper, u + pltpu.roll(u, 126, 1), v + pltpu.roll(v, 2, 1)))
         r1 = pltpu.roll(cc[1], 64, 1)
         r3 = pltpu.roll(cc[3], 64, 1)
         v0 = jnp.where(
@@ -554,38 +575,56 @@
         for i, v in enumerate((v0, v1, v2)):
             tok[group, 8 * t : 8 * t + 8, :, 128 * i : 128 * i + 128] = v.reshape(8, 8, 128)
 
-    def own_copy(d, sending):
-        a, b = FARTHEST[d - 1]
-        j = tile_at((a, b))
-        at = tl if sending else tile_at((4 - a, 4 - b))
-        return remote(tok.at[0, j], trecv.at[0, at], tks.at[0, d], tkr.at[0, at], (tm, j))
-
-    def span_copy(d, sending):
-        a, b = ((FARTHEST + ((0, 0),)))[d]
-        j = tile_at((a, b))
-        at = tl if sending else tile_at((4 - a, 4 - b))
-        return remote(tok.at[1, j], trecv.at[1, at], tks.at[1, d], tkr.at[1, at], (below, j))
-
-    left_side(0)
-    conv(0, 0, 1)
-    left_side(1)
-    conv(1, 0, 0)
+    def own_copy(j, at):
+        return remote(tok.at[0, j], trecv.at[0, at], tks.at[0, j], tkr.at[0, at], (tm, j))
+
+    def span_copy(j, at):
+        return remote(tok.at[1, j], trecv.at[1, at], tks.at[1, j], tkr.at[1, at], (below, j))
+
+    def owners(t):
+        return tuple(
+            8 * t + 4 * lax.rem(x + a, 2) + lax.rem(y + b, 4) for b in (2, 1, 3, 0) for a in (1, 0)
+        )
+
+    def send_span(t):
+        for j in owners(t):
+            span_copy(j, tl).start()
+
+    def send_own(t):
+        for j in owners(t):
+
+            @pl.when(j != tl)
+            def _(j=j):
+                own_copy(j, tl).start()
+
+    left_side(0, (1, 2))
+    conv_middle(0, 0, 1)
+    left_side(0, (0, 3))
+    conv_ends(0, 0, 1)
+    left_side(1, (1, 2))
+    conv_middle(1, 0, 0)
+    left_side(1, (0, 3))
     tokens(1, 0, ((0, 0),))
+    send_span(0)
+    conv_ends(1, 0, 0)
     tokens(1, 1, ((0, 1), (1, 0)))
-    for d in range(16):
-        span_copy(d, True).start()
-    conv(0, 2, 2)
-    conv(1, 1, 2)
+    send_span(1)
+    conv_middle(0, 2, 2)
+    conv_ends(0, 2, 2)
+    conv_middle(1, 1, 2)
+    conv_ends(1, 1, 2)
     tokens(0, 0, ((0, 2), (1, 1)))
     tokens(0, 1, ((1, 2),))
-    for d in range(1, 16):
-        own_copy(d, True).start()
+    send_own(0)
+    send_own(1)
     trecv[0, tl] = tok[0, tl]
 
-    for d in range(16):
-        span_copy(d, False).wait_recv()
-    for d in range(1, 16):
-        own_copy(d, False).wait_recv()
+    for place in FARTHEST + ((0, 0),):
+        j = tile_at(place)
+        span_copy(j, j).wait_recv()
+    for place in FARTHEST:
+        j = tile_at(place)
+        own_copy(j, j).wait_recv()
 
     def assemble():
         ln = iota((8, 128), 1)
@@ -629,10 +668,10 @@
             z_copy(half, r, d).wait_send()
         for d in range(1, 16):
             stat_copy(half, d).wait_send()
-    for d in range(1, 16):
-        own_copy(d, True).wait_send()
-    for d in range(16):
-        span_copy(d, True).wait_send()
+    for place in FARTHEST:
+        own_copy(tile_at(place), tl).wait_send()
+    for place in FARTHEST + ((0, 0),):
+        span_copy(tile_at(place), tl).wait_send()
 
 
 def body(pix_grad, frame_ids, pre_norm, gain, bias, out_weight, conv_weight, in_weight):
@@ -678,12 +717,18 @@
             pltpu.VMEM((8, 128), F32),
             pltpu.VMEM((8, BLK), F32),
             pltpu.VMEM((27, 96, 128), F32),
-            pltpu.VMEM((6 * BLK, 2 * BLK), BF16),
-            pltpu.VMEM((320, 6 * BLK), BF16),
-            pltpu.VMEM((320, 6 * BLK), BF16),
+            pltpu.VMEM((2 * BLK, BLK), BF16),
+            pltpu.VMEM((2 * BLK, 2 * BLK), BF16),
+            pltpu.VMEM((2 * BLK, BLK), BF16),
+            pltpu.VMEM((2, 320, 2 * BLK), BF16),
+            pltpu.VMEM((2, 320, 2 * BLK), BF16),
+            pltpu.VMEM((2, 320, 2 * BLK), BF16),
+            pltpu.VMEM((640, BLK), F32),
             pltpu.VMEM((640, 2 * BLK), F32),
+            pltpu.VMEM((640, BLK), F32),
             pltpu.VMEM((2, 16, 8, BLK), F32),
             pltpu.VMEM((2, 16, 8, BLK), F32),
+            pltpu.SemaphoreType.REGULAR,
             dma,
             dma((PIECES,)),
             dma,

time: 40.6 us -> 39.3 us (0.968)
  Pallas kernels: 38.7 us -> 37.6 us
    pallas_call x1, Pallas kernels: 38.7 us -> 37.6 us  [body(): pl.pallas_call(kernel, out_shape=jax.ShapeDtypeStruct((8, 5120), F32), in...]
where the time goes in v6:
time: 39.3 us; the launch traced here: 39 us
  Pallas kernels  37.6 us (96%)
  local copies, waits for them, and re-layouts  0.67 us (2%)
  between operations  0.66 us (2%)
    pallas_call x1, Pallas kernels, body(): pl.pallas_call(kernel, out_shape=jax.ShapeDtypeStruct((8, 5120), F32), in...  37.6 us

profile of v6, /device:TPU:1, one launch (start us, length us, event | category | flops | bytes accessed | tf_op | source)
XLA Modules:
  0.0 39.0 jit_solution(12290992975352888566)
XLA Ops:
  0.7 37.6 %shard_map.82 = f32[8,5120]{1,0:T(8,128)S(1)} custom-call(bf16[1,3,320,256]{3,2,1,0:T(8,128)(2,1)} %bitcast.4, s32[1]{0:T(128)S(6)} %copy.10.fid, bf16[2,256,1920]{2,1,0:T(8,128)(2,1)} %x_hbm.1, f32[1,96]{1,0:T(1,128)} %bitcast.6, f32[1,96]{1,0:T(1,128)} %bitcast.7, bf16[3,96]{1,0:T(4,128)(2,1)} %bitcast.5, bf16[27,96,384]{2,1,0:T(8,128)(2,1)} %cw_hbm.1, ...), custom_call_target="tpu_custom_call" | custom-call | tf_op jit(solution)/shard_map/pallas_call | solution.py:689
  38.3 0.7 %copy.11 = f32[8,5120]{1,0:T(8,128)} copy(f32[8,5120]{1,0:T(8,128)S(1)} %shard_map.82) | data formatting | bytes 327680

commit v7 on v6

--- a/solution.py
+++ b/solution.py
@@ -134,6 +134,29 @@
 
     pix_cp = pltpu.make_async_copy(pix_hbm.at[0], pixv, pix_sem)
     pix_cp.start()
+    def pack():
+        r = iota((256, 240), 0)
+        m = iota((256, 240), 1)
+        slot = lax.rem(r, 32)
+        col = 20 * lax.div(r, 64) + 10 * lax.div(lax.rem(r, 64), 32) + lax.rem(slot, 10)
+        hit = (slot < 30) & (m == 80 * lax.div(slot, 10) + col)
+        pick = jnp.where(hit, 1.0, 0.0).astype(BF16)
+        frame_id = fid[0].astype(F32)
+        spare = lax.rem(iota((256, 256), 0), 32) >= 30
+        pix_cp.wait()
+        for n in range(4):
+            stack = jnp.concatenate(
+                [pixv[k, 80 * n : 80 * n + 80, :] for k in range(3)], axis=0
+            )
+            rows = jnp.dot(pick, stack, preferred_element_type=F32)
+            rows = jnp.where(spare, frame_id, rows).astype(BF16)
+            for jj in range(4):
+                for ch in range(2):
+                    sbuf[ch, 4 * n + jj] = rows[
+                        64 * jj : 64 * jj + 64, 128 * ch : 128 * ch + 128
+                    ]
+
+    pack()
     x_cps = []
     for f in range(2):
         for b in range(5):
@@ -151,30 +174,6 @@
         small_cps.append(cp)
     cw_cp = pltpu.make_async_copy(cw_hbm, cwv, cw_sem)
     cw_cp.start()
-
-    def pack():
-        frame_id = fid[0].astype(F32)
-        r = iota((256, 240), 0)
-        m = iota((256, 240), 1)
-        slot = lax.rem(r, 32)
-        col = 20 * lax.div(r, 64) + 10 * lax.div(lax.rem(r, 64), 32) + lax.rem(slot, 10)
-        hit = (slot < 30) & (m == 80 * lax.div(slot, 10) + col)
-        pick = jnp.where(hit, 1.0, 0.0).astype(BF16)
-        spare = lax.rem(iota((256, 256), 0), 32) >= 30
-        for n in range(4):
-            stack = jnp.concatenate(
-                [pixv[k, 80 * n : 80 * n + 80, :] for k in range(3)], axis=0
-            )
-            rows = jnp.dot(pick, stack, preferred_element_type=F32)
-            rows = jnp.where(spare, frame_id, rows).astype(BF16)
-            for jj in range(4):
-                for ch in range(2):
-                    sbuf[ch, 4 * n + jj] = rows[
-                        64 * jj : 64 * jj + 64, 128 * ch : 128 * ch + 128
-                    ]
-
-    pix_cp.wait()
-    pack()
     def strip_copy(half, r, d):
         j = tl if d == 0 else tile_at(PEERS[d - 1])
         h = lax.rem(c + r, 2)
@@ -601,11 +600,11 @@
     conv_middle(0, 0, 1)
     left_side(0, (0, 3))
     conv_ends(0, 0, 1)
+    tokens(1, 0, ((0, 0),))
+    send_span(0)
     left_side(1, (1, 2))
     conv_middle(1, 0, 0)
     left_side(1, (0, 3))
-    tokens(1, 0, ((0, 0),))
-    send_span(0)
     conv_ends(1, 0, 0)
     tokens(1, 1, ((0, 1), (1, 0)))
     send_span(1)
@@ -614,8 +613,8 @@
     conv_middle(1, 1, 2)
     conv_ends(1, 1, 2)
     tokens(0, 0, ((0, 2), (1, 1)))
+    send_own(0)
     tokens(0, 1, ((1, 2),))
-    send_own(0)
     send_own(1)
     trecv[0, tl] = tok[0, tl]
 

time: 39.3 us -> 39.2 us (level); the launches traced: 39 us -> 38.4 us
  Pallas kernels: 37.6 us -> 37.1 us
    pallas_call x1, Pallas kernels: 37.6 us -> 37.1 us  [body(): pl.pallas_call(kernel, out_shape=jax.ShapeDtypeStruct((8, 5120), F32), in...]
where the time goes in v7:
time: 39.2 us; the launch traced here: 38.4 us
  Pallas kernels  37.1 us (95%)
  local copies, waits for them, and re-layouts  0.67 us (2%)
  between operations  0.66 us (2%)
    pallas_call x1, Pallas kernels, body(): pl.pallas_call(kernel, out_shape=jax.ShapeDtypeStruct((8, 5120), F32), in...  37.1 us

profile of v7, /device:TPU:1, one launch (start us, length us, event | category | flops | bytes accessed | tf_op | source)
XLA Modules:
  0.0 38.4 jit_solution(1935616409580862683)
XLA Ops:
  0.7 37.1 %shard_map.82 = f32[8,5120]{1,0:T(8,128)S(1)} custom-call(bf16[1,3,320,256]{3,2,1,0:T(8,128)(2,1)} %bitcast.4, s32[1]{0:T(128)S(6)} %copy.10.fid, bf16[2,256,1920]{2,1,0:T(8,128)(2,1)} %x_hbm.1, f32[1,96]{1,0:T(1,128)} %bitcast.6, f32[1,96]{1,0:T(1,128)} %bitcast.7, bf16[3,96]{1,0:T(4,128)(2,1)} %bitcast.5, bf16[27,96,384]{2,1,0:T(8,128)(2,1)} %cw_hbm.1, ...), custom_call_target="tpu_custom_call" | custom-call | tf_op jit(solution)/shard_map/pallas_call | solution.py:688
  37.7 0.7 %copy.11 = f32[8,5120]{1,0:T(8,128)} copy(f32[8,5120]{1,0:T(8,128)S(1)} %shard_map.82) | data formatting | bytes 327680

commit v8 on v7

--- a/solution.py
+++ b/solution.py
@@ -157,6 +157,33 @@
                     ]
 
     pack()
+    def strip_copy(half, r, d):
+        j = tl if d == 0 else tile_at(PEERS[d - 1])
+        h = lax.rem(c + r, 2)
+        rows = pl.ds(32 * half, 32)
+        return remote(
+            sbuf.at[h, j, rows],
+            rbuf.at[r, d, rows],
+            s1s.at[half, r, d],
+            s1r.at[half, r, d],
+            (2 * z + h, j),
+        )
+
+    strips = tuple((r, d) for d in range(1, 16) for r in range(2)) + ((1, 0),)
+
+    def strips_sent(some):
+        for half in range(2):
+            for r, d in some:
+                strip_copy(half, r, d).start()
+
+    pl.semaphore_wait(barrier, 12 + 6 + 1)
+    for place in ((2, 0), (1, 0), (3, 0)):
+        pl.semaphore_signal(
+            ready_sem, inc=1, device_id=(tm, tile_at(place)), device_id_type=MESH
+        )
+    strips_sent(strips[0:12] + strips[-1:])
+    rbuf[0, 0] = sbuf[c, tl]
+
     x_cps = []
     for f in range(2):
         for b in range(5):
@@ -174,32 +201,6 @@
         small_cps.append(cp)
     cw_cp = pltpu.make_async_copy(cw_hbm, cwv, cw_sem)
     cw_cp.start()
-    def strip_copy(half, r, d):
-        j = tl if d == 0 else tile_at(PEERS[d - 1])
-        h = lax.rem(c + r, 2)
-        rows = pl.ds(32 * half, 32)
-        return remote(
-            sbuf.at[h, j, rows],
-            rbuf.at[r, d, rows],
-            s1s.at[half, r, d],
-            s1r.at[half, r, d],
-            (2 * z + h, j),
-        )
-
-    strips = tuple((r, d) for d in range(1, 16) for r in range(2)) + ((1, 0),)
-
-    def strips_sent(some):
-        for half in range(2):
-            for r, d in some:
-                strip_copy(half, r, d).start()
-
-    pl.semaphore_wait(barrier, 12 + 6 + 1)
-    for place in ((2, 0), (1, 0), (3, 0)):
-        pl.semaphore_signal(
-            ready_sem, inc=1, device_id=(tm, tile_at(place)), device_id_type=MESH
-        )
-    strips_sent(strips[0:12] + strips[-1:])
-    rbuf[0, 0] = sbuf[c, tl]
 
     pl.semaphore_wait(ready_sem, 3)
     strips_sent(strips[12:30])

time: 39.2 us -> 39.2 us (level)
  no operation moved by 1% of the time
where the time goes in v8:
time: 39.2 us; the launch traced here: 38.4 us
  Pallas kernels  37.1 us (95%)
  local copies, waits for them, and re-layouts  0.67 us (2%)
  between operations  0.66 us (2%)
    pallas_call x1, Pallas kernels, body(): pl.pallas_call(kernel, out_shape=jax.ShapeDtypeStruct((8, 5120), F32), in...  37.1 us

profile of v8, /device:TPU:1, one launch (start us, length us, event | category | flops | bytes accessed | tf_op | source)
XLA Modules:
  0.0 38.4 jit_solution(16811730631505905038)
XLA Ops:
  0.7 37.1 %shard_map.82 = f32[8,5120]{1,0:T(8,128)S(1)} custom-call(bf16[1,3,320,256]{3,2,1,0:T(8,128)(2,1)} %bitcast.4, s32[1]{0:T(128)S(6)} %copy.10.fid, bf16[2,256,1920]{2,1,0:T(8,128)(2,1)} %x_hbm.1, f32[1,96]{1,0:T(1,128)} %bitcast.6, f32[1,96]{1,0:T(1,128)} %bitcast.7, bf16[3,96]{1,0:T(4,128)(2,1)} %bitcast.5, bf16[27,96,384]{2,1,0:T(8,128)(2,1)} %cw_hbm.1, ...), custom_call_target="tpu_custom_call" | custom-call | tf_op jit(solution)/shard_map/pallas_call | solution.py:689
  37.7 0.7 %copy.11 = f32[8,5120]{1,0:T(8,128)} copy(f32[8,5120]{1,0:T(8,128)S(1)} %shard_map.82) | data formatting | bytes 327680
